TPU v7x, 256 devices: a whole 4x4x8 slice. The times are simulated.
256 devices in a mesh: term: 8 (over y, core), sector: 32 (over z, x).
Axes of the slice: x: 4, y: 4, z: 8, core: 2. Of those that a mesh axis runs over, the one named last changes fastest.
Arguments:
- wavefunction: bfloat16 [32, 3, 256, 256], P('sector'), may hold values from -6 to 6
- left_operators: bfloat16 [32, 256, 256, 256], P('sector', 'term'), may hold values from -0.0234375 to 0.0234375
- right_operators: bfloat16 [32, 256, 256, 256], P('sector', 'term'), may hold values from -0.375 to 0.375
- target_sector: int32 [32, 256, 1], P('sector', 'term'), may hold values from 0 to 31; in each aligned block of 32 rows (0 to 31, 32 to 63, ..., all dimensions but the last counted through in order) at most 2 rows name the same one
Outputs:
- sigma_blocks: float32 [32, 3, 256, 256], P('sector', None, 'term')
Inputs may be any that keep to these rules, and one draw needn't show every extreme that they name: `target_sector`: in each aligned block of 32 terms of one source sector no target appears more than 2 times, and some block reaches 2.
All inputs are finite; a program needn't handle non-finite values.
Results may differ from a plain program's by a relative error of at most 0.017.
Values may be sent and summed in bfloat16 or wider, within the bound.
No kernel may reach another device: no remote copies, remote signals or barrier semaphores. Data moves between devices by JAX's collectives and lax.ppermute only.
A program may use at most 128 MiB of HBM per device.

v0:
```python
import math

import jax
import jax.numpy as jnp
from jax import lax
from jax.sharding import PartitionSpec as P


def body(wavefunction, left_operators, right_operators, target_sector):
    local_wavefunction = wavefunction[0]
    left_block = left_operators[0]
    right_block = right_operators[0]
    num_items = left_block.shape[0]
    block_width = left_block.shape[1]
    vectors = local_wavefunction.shape[0]
    per_turn = math.gcd(num_items, 8)

    def one_batch(operands):
        left_factor, right_factor = operands
        partial_contraction = jnp.einsum(
            "dsk,owk->odsw", local_wavefunction, right_factor, preferred_element_type=jnp.float32
        ).astype(jnp.bfloat16)
        return jnp.einsum(
            "qdk,qfks->qfds", left_factor, partial_contraction, preferred_element_type=jnp.float32
        ).astype(jnp.bfloat16)

    shaped = (num_items // per_turn, per_turn, block_width, block_width)
    products = lax.map(one_batch, (left_block.reshape(shaped), right_block.reshape(shaped)))
    products = products.reshape(num_items, vectors, block_width, block_width)
    targets_here = target_sector[0, :, 0]
    sectors = lax.axis_size("sector")
    term_count = lax.axis_size("term")
    row_share = block_width // term_count
    capacity = 2 * num_items // sectors
    positions = jnp.arange(num_items)
    same_target = targets_here[:, None] == targets_here[None, :]
    earlier = positions[None, :] < positions[:, None]
    slot_rank = jnp.sum(jnp.where(same_target & earlier, 1, 0), axis=1)
    slot_item = targets_here * capacity + slot_rank
    slot_ids = jnp.arange(sectors * capacity)
    matches = slot_ids[:, None] == slot_item[None, :]
    filled = jnp.any(matches, axis=1)
    source = jnp.sum(jnp.where(matches, positions[None, :], 0), axis=1)
    buffer = jnp.where(filled[:, None, None, None], products[source], jnp.zeros((), jnp.bfloat16))
    received = lax.all_to_all(buffer, "sector", split_axis=0, concat_axis=0, tiled=True)
    received = received.reshape((sectors, capacity) + received.shape[1:])
    source_sums = jnp.sum(received.astype(jnp.float32), axis=1)
    source_sums = lax.optimization_barrier(source_sums.astype(jnp.bfloat16))
    partial_value = jnp.sum(source_sums.astype(jnp.float32), axis=0)
    grand_total = lax.psum(partial_value.astype(jnp.bfloat16), "term").astype(jnp.float32)
    own_rows = lax.dynamic_slice_in_dim(
        grand_total, lax.axis_index("term") * row_share, row_share, 1
    )
    return own_rows[None]


def solution(mesh):
    return jax.shard_map(
        body,
        mesh=mesh,
        in_specs=(
            P("sector", None, None, None),
            P("sector", "term", None, None),
            P("sector", "term", None, None),
            P("sector", "term", None),
        ),
        out_specs=P("sector", None, "term", None),
        check_vma=False,
    )
```

profile of v0, /device:TPU:6, one launch (start us, length us, event | category | flops | bytes accessed | tf_op | source)
XLA Modules:
  0.0 713.4 jit_solution(11020837292445263794)
XLA Ops:
  6.5 0.0 all-reduce.2.cloned.1.call-start
  6.5 0.9 select_reduce_fusion.1
  7.4 0.7 multiply_add_fusion
  8.1 0.1 select_reduce_fusion
  8.2 0.1 fusion.17
  8.3 20.9 %while.10 = (s32[]{:T(128)}, bf16[4,8,3,256,256]{3,4,2,1,0:T(8,128)(2,1)}, bf16[4,8,256,256]{3,2,1,0:T(8,128)(2,1)}, bf16[3,256,256]{2,1,0:T(8,128)(2,1)}, bf16[4,8,256,256]{3,2,1,0:T(8,128)(2,1)}, /*index=5*/s32[]{:T(128)}) while((s32[]{:T(128)}, bf16[4,8,3,256,256]{3,4,2,1,0:T(8,128)(2,1)}, bf16[4,8,256,256]{3,2,1,0:T(8,128)(2,1)}, ...), condition=%wide.region_3.4_spmd, body=%wide.region_2.3_spmd.sunk | while | flops 1613758464 | bytes 5637709 | solution.py:28
  8.3 5.3 bitcast_dynamic-update-slice_fusion.2
  13.6 5.3 bitcast_dynamic-update-slice_fusion.2
  18.8 5.1 bitcast_dynamic-update-slice_fusion.2
  24.0 5.2 bitcast_dynamic-update-slice_fusion.2
  29.2 14.8 %gather_fusion = bf16[64,3,256,256]{2,3,1,0:T(8,128)(2,1)} fusion(bf16[32,3,256,256]{2,3,1,0:T(8,128)(2,1)} %bitcast.49, s32[1024]{0:T(1024)S(1)} %pad_clamp_fusion), kind=kCustom, calls=%fused_computation | custom fusion | bytes 50331904 | tf_op jit(solution)/shard_map/gather | solution.py:44
  44.1 12.2 %broadcast_select_fusion = bf16[64,3,256,256]{2,3,1,0:T(8,128)(2,1)S(1)} fusion(bf16[64,3,256,256]{2,3,1,0:T(8,128)(2,1)} %gather_fusion, pred[64]{0:T(512)(128)(4,1)S(1)} %fusion.17), kind=kLoop, calls=%fused_computation.13 | loop fusion | flops 12582912 | bytes 50331712 | tf_op jit(solution)/shard_map/jit(_where)/select_n | solution.py:44
  56.3 556.3 %all_to_all.5 = bf16[64,3,256,256]{2,3,1,0:T(8,128)(2,1)} all-to-all(bf16[64,3,256,256]{2,3,1,0:T(8,128)(2,1)S(1)} %broadcast_select_fusion), channel_id=1, replica_groups=mesh['term'=8,'sector'=32] {'sector'}, dimensions={0} | all-to-all | bytes 50331648 | tf_op jit(solution)/shard_map/all_to_all | solution.py:45
  612.6 21.2 %bitcast_reduce_fusion = bf16[32,3,256,256]{2,3,1,0:T(8,128)(2,1)} fusion(bf16[64,3,256,256]{2,3,1,0:T(8,128)(2,1)} %all_to_all.5), kind=kLoop, calls=%fused_computation.12 | loop fusion | flops 6291456 | bytes 37748736 | tf_op jit(solution)/shard_map/reduce_sum | solution.py:47
  633.8 8.3 %reduce_sum.48 = bf16[3,256,256]{1,2,0:T(8,128)(2,1)} reduce(bf16[32,3,256,256]{2,3,1,0:T(8,128)(2,1)} %bitcast_reduce_fusion, bf16[]{:T(256)} %constant.19.clone.1), dimensions={0}, to_apply=%region_6.7 | reduce | flops 6094848 | bytes 12976130 | tf_op jit(solution)/shard_map/reduce_sum | solution.py:49
  642.1 0.0 all-reduce.2.cloned.1.call-update
  642.1 62.6 %all-reduce.2.cloned.1.call-done = bf16[3,256,256]{1,2,0:T(8,128)(2,1)} async-done(((bf16[3,256,256]{1,2,0:T(8,128)(2,1)}), bf16[3,256,256]{1,2,0:T(8,128)(2,1)}) %all-reduce.2.cloned.1.call-update) | async-done | bytes 393232 | tf_op jit(solution)/shard_map/psum | solution.py:50
  704.8 1.0 dynamic-slice_convert_fusion
  705.8 0.8 copy.6
  (3 shorter events, 0.0 us)
Async XLA Ops:
  6.5 698.2 %all-reduce.2.cloned.1.call-start = ((), (), s32[]{:S(2)}) async-start(), calls=%async_computation.1 | async-start | bytes 786432 | tf_op jit(solution)/shard_map/psum | solution.py:50
Sparse Core Ops, SparseCore 0:
  642.3 62.4 all-reduce.1
where the time goes:
time: 714 us; the launch traced here: 713 us
  blocking collectives  556 us (78%)
  waiting for transfers between devices  62.6 us (9%)
  other arithmetic  44.5 us (6%)
  matrix products  20.9 us (3%)
  local copies, waits for them, and re-layouts  15.6 us (2%)
  between operations  13.4 us (2%)
    all_to_all x1, blocking collectives, body(): lax.all_to_all(buffer, 'sector', split_axis=0, concat_axis=0, tiled=True)  556 us
    psum x1, waiting for transfers between devices, body(): lax.psum(partial_value.astype(jnp.bfloat16), 'term').astype(jnp.float32)  62.6 us
    reduce_sum x1, other arithmetic, body(): source_sums = jnp.sum(received.astype(jnp.float32), axis=1)  21.2 us
    dot_general x4, matrix products, one_batch(): jnp.einsum('qdk,qfks->qfds', left_factor, partial_contraction, preferred_...  20.9 us
    gather x1, local copies, waits for them, and re-layouts, body(): products[source]  14.8 us
  transfers between devices with their start and end apart: 1, of which 1 were waited for; matrix products, arithmetic and copies ran while one was open for 0% of the time, Pallas kernels for 0%

commit v1 on v0

v1 whole, which is shorter than its diff:
```python
import functools

import jax
import jax.numpy as jnp
import numpy as np
from jax import lax
from jax.experimental import pallas as pl
from jax.experimental.pallas import tpu as pltpu
from jax.sharding import Mesh, PartitionSpec as P

AXES = ("y", "c", "z", "x")
SIZES = (4, 2, 8, 4)
K = 256
TERMS = 32
ROWS = 32
PER_STEP = 4


def gray(n):
    return n ^ (n >> 1)


def ring_slot(distance, core):
    return gray(jnp.where(core == 0, (4 - distance) & 3, distance))


def ring_distance(slot, core):
    distance = gray(slot)
    return jnp.where(core == 0, (4 - distance) & 3, distance)


def ring_flip(step, core):
    return 1 if step == core else 3


def layout_z(b_z, b_x, z, x, c):
    distance = ((b_z - c) & 7) ^ ((z - c) & 7)
    slot = (distance & 1) * 4 + ring_slot(distance >> 1, c)
    return slot * 16 + b_x


def layout_x(b_z, b_x, z, x, c):
    return ring_slot(b_x ^ x, c) * 32 + b_z


def layout_y(b_z, b_x, z, x, c):
    return (b_x ^ x) * 8 + b_z


LAYOUTS = {
    "z": (layout_z, 4, lambda j, y, c: j),
    "x": (layout_x, 8, lambda j, y, c: y ^ j),
    "y": (layout_y, 32, lambda j, y, c: y ^ ring_distance(j, c)),
}


def products_kernel(first, place_ref, psi_ref, left_ref, right_ref, keep_ref, send_ref):
    layout, stride, row_owner = LAYOUTS[first]
    step = pl.program_id(0)
    y, c, z, x = (place_ref[TERMS + i] for i in range(4))

    @pl.when(step == 0)
    def _():
        keep_ref[...] = jnp.zeros_like(keep_ref)
        send_ref[...] = jnp.zeros_like(send_ref)

    cores = (c, 1 - c)
    owners = [(row_owner(j, y, core) * 2 + core) * ROWS for core in cores for j in range(4)]
    rows = [pl.multiple_of(o, ROWS) for o in owners]
    psi = psi_ref[...]
    left = jnp.concatenate([left_ref[t, pl.ds(r, ROWS), :] for t in range(PER_STEP) for r in rows], axis=0)
    turned = jnp.dot(left, psi, preferred_element_type=jnp.float32).astype(jnp.bfloat16)
    for t in range(PER_STEP):
        product = lax.dot_general(
            turned[t * K:(t + 1) * K], right_ref[t], (((1,), (1,)), ((), ())), preferred_element_type=jnp.float32
        )
        target = place_ref[step * PER_STEP + t]
        for part, ref in enumerate((keep_ref, send_ref)):
            base = layout(target >> 2, target & 3, z, x, cores[part])
            for j in range(4):
                value = product[(part * 4 + j) * ROWS:(part * 4 + j + 1) * ROWS]
                at = base + j * stride
                ref[at] = (ref[at].astype(jnp.float32) + value).astype(jnp.bfloat16)


def local_sums(first, place, psi, left, right):
    block = pl.BlockSpec((PER_STEP, K, K), lambda i, place: (i, 0, 0))
    whole = pl.BlockSpec((128, ROWS, K), lambda i, place: (0, 0, 0))
    shape = jax.ShapeDtypeStruct((128, ROWS, K), jnp.bfloat16)
    return pl.pallas_call(
        functools.partial(products_kernel, first),
        grid_spec=pltpu.PrefetchScalarGridSpec(
            num_scalar_prefetch=1,
            grid=(TERMS // PER_STEP,),
            in_specs=[pl.BlockSpec((K, K), lambda i, place: (0, 0)), block, block],
            out_specs=[whole, whole],
        ),
        out_shape=[shape, shape],
        compiler_params=pltpu.CompilerParams(vmem_limit_bytes=24 * 2**20),
        cost_estimate=pl.CostEstimate(flops=4 * TERMS * K**3, bytes_accessed=13 * 2**20, transcendentals=0),
    )(place, psi, left, right)


def permutation(move):
    pairs = []
    for index in range(256):
        place = [int(v) for v in np.unravel_index(index, SIZES)]
        pairs.append((index, int(np.ravel_multi_index(move(*place), SIZES))))
    return pairs


def core_swap(a):
    return lax.ppermute(a, AXES, permutation(lambda y, c, z, x: (y, 1 - c, z, x)))


def ring_swap(a, axis, step):
    if axis == "x":
        return lax.ppermute(a, AXES, permutation(lambda y, c, z, x: (y, c, z, x ^ ring_flip(step, c))))
    return lax.ppermute(a, AXES, permutation(lambda y, c, z, x: (y ^ ring_flip(step, c), c, z, x)))


def far_swap(a, axis, distance):
    if axis == "x":
        return lax.ppermute(a, AXES, permutation(lambda y, c, z, x: (y, c, z, x ^ distance)))
    return lax.ppermute(a, AXES, permutation(lambda y, c, z, x: (y ^ distance, c, z, x)))


def z_swap(a, step):
    def move(y, c, z, x):
        flip = 1 if step == 0 else 2 * ring_flip(step - 1, c)
        return (y, c, ((((z - c) % 8) ^ flip) + c) % 8, x)

    return lax.ppermute(a, AXES, permutation(move))


def total(*arrays):
    value = arrays[0].astype(jnp.float32)
    for a in arrays[1:]:
        value = value + a.astype(jnp.float32)
    return value


def rounded(*arrays):
    return total(*arrays).astype(jnp.bfloat16)


def halve_ring(parts, axis):
    first = ring_swap(rounded(*(a[2:] for a in parts)), axis, 0)
    second = ring_swap(rounded(*(a[1] for a in parts), first[1]), axis, 1)
    return [*(a[0] for a in parts), first[0], second]


def direct_ring(parts, axis):
    mine = rounded(*parts)
    return [mine[0]] + [far_swap(mine[d], axis, d) for d in (1, 2, 3)]


def halve_z(parts):
    first = z_swap(rounded(*(a[4:] for a in parts)), 0)
    parts = [*(a[:4] for a in parts), first]
    second = z_swap(rounded(*(a[2:] for a in parts)), 1)
    third = z_swap(rounded(*(a[1] for a in parts), second[1]), 2)
    return [*(a[0] for a in parts), second[0], third]


def body(wavefunction, left_operators, right_operators, target_sector):
    psi, left, right = wavefunction[0], left_operators[0], right_operators[0]
    here = jnp.stack([lax.axis_index(a) for a in AXES]).astype(jnp.int32)
    place = jnp.concatenate([target_sector[0, :, 0], here])
    shape = (ROWS, K)

    def part(first, vector, dims):
        keep, send = local_sums(first, place, psi[vector], left, right)
        return [keep.reshape(dims + shape), core_swap(send).reshape(dims + shape)]

    part_z = part("z", 0, (8, 4, 4))
    part_x = part("x", 1, (4, 4, 8))
    part_y = part("y", 2, (4, 4, 8))
    part_z = halve_z(part_z)
    part_x = halve_ring(part_x, "x")
    part_y = halve_ring(part_y, "y")
    part_x = direct_ring(part_x, "y")
    part_y = direct_ring(part_y, "x")
    spread = lax.all_to_all(rounded(*part_z).reshape((16,) + shape), ("y", "x"), 0, 0, tiled=True)
    out_z = jnp.sum(spread.astype(jnp.float32), axis=0)
    both = jnp.stack([rounded(*part_x), rounded(*part_y)], axis=1)
    spread = lax.all_to_all(both, "z", 0, 0, tiled=True)
    out_xy = jnp.sum(spread.astype(jnp.float32), axis=0)
    return jnp.concatenate([out_z[None], out_xy], axis=0)[None]


def solution(mesh):
    fine = Mesh(np.array(mesh.devices).reshape(SIZES), AXES)
    return jax.shard_map(
        body,
        mesh=fine,
        in_specs=(
            P(("z", "x"), None, None, None),
            P(("z", "x"), ("y", "c"), None, None),
            P(("z", "x"), ("y", "c"), None, None),
            P(("z", "x"), ("y", "c"), None),
        ),
        out_specs=P(("z", "x"), None, ("y", "c"), None),
        check_vma=False,
    )
```

time: 714 us -> 108 us (0.15)
  blocking collectives: 556 us -> 0 us
  other arithmetic: 44.5 us -> 6.16 us
  starting transfers between devices: 0.01 us -> 35.4 us
  matrix products: 20.9 us -> 0 us
  waiting for transfers between devices: 62.6 us -> 42.9 us
  Pallas kernels: 0 us -> 15.8 us
  between operations: 13.4 us -> 0.21 us
  local copies, waits for them, and re-layouts: 15.6 us -> 6.23 us
    all_to_all x1 -> x0, blocking collectives: 556 us -> none  [body(): lax.all_to_all(buffer, 'sector', split_axis=0, concat_axis=0, tiled=True)]
    psum x1 -> x0, waiting for transfers between devices: 62.6 us -> none  [body(): lax.psum(partial_value.astype(jnp.bfloat16), 'term').astype(jnp.float32)]
    reduce_sum x4 -> x2, other arithmetic: 30.5 us -> 0.08 us  [the longest x1 0.04 us: body(): out_z = jnp.sum(spread.astype(jnp.float32), axis=0)]
    ppermute x0 -> x16, waiting for transfers between devices: none -> 27.1 us  [the longest x3 24.1 us: z_swap(): return lax.ppermute(a, AXES, permutation(move))]
    ppermute x0 -> x16, starting transfers between devices: none -> 25.8 us  [the longest x3 11 us: z_swap(): return lax.ppermute(a, AXES, permutation(move))]
    dot_general x4 -> x0, matrix products: 20.9 us -> none  [one_batch(): jnp.einsum('qdk,qfks->qfds', left_factor, partial_contraction, preferred_...]
    all_to_all x0 -> x2, waiting for transfers between devices: none -> 15.8 us  [the longest x1 10.4 us: body(): spread = lax.all_to_all(both, 'z', 0, 0, tiled=True)]
    pallas_call x0 -> x3, Pallas kernels: none -> 15.8 us  [local_sums(): pl.pallas_call(functools.partial(products_kernel, first), grid_spec=pltpu...]
  transfers between devices with their start and end apart: 1 -> 18, of which waited for: 1 -> 8; matrix products, arithmetic and copies ran while one was open for 0% -> 5% of each run, Pallas kernels for 0% -> 10%
where the time goes in v1:
time: 108 us; the launch traced here: 107 us
  waiting for transfers between devices  42.9 us (40%)
  starting transfers between devices  35.4 us (33%)
  Pallas kernels  15.8 us (15%)
  local copies, waits for them, and re-layouts  6.23 us (6%)
  other arithmetic  6.16 us (6%)
    ppermute x3, waiting for transfers between devices, z_swap(): return lax.ppermute(a, AXES, permutation(move))  24.1 us
    pallas_call x3, Pallas kernels, local_sums(): pl.pallas_call(functools.partial(products_kernel, first), grid_spec=pltpu...  15.8 us
    ppermute x3, starting transfers between devices, z_swap(): return lax.ppermute(a, AXES, permutation(move))  11 us
    all_to_all x1, waiting for transfers between devices, body(): spread = lax.all_to_all(both, 'z', 0, 0, tiled=True)  10.4 us
    all_to_all x1, starting transfers between devices, body(): lax.all_to_all(rounded(*part_z).reshape((16,) + shape), ('y', 'x'), 0, 0,...  6.14 us
    all_to_all x1, waiting for transfers between devices, body(): lax.all_to_all(rounded(*part_z).reshape((16,) + shape), ('y', 'x'), 0, 0,...  5.47 us
    ppermute x3, starting transfers between devices, far_swap(): lax.ppermute(a, AXES, permutation(lambda y, c, z, x: (y ^ distance, c, z,...  4.79 us
    ppermute x2, starting transfers between devices, ring_swap(): lax.ppermute(a, AXES, permutation(lambda y, c, z, x: (y ^ ring_flip(step,...  4.77 us
  transfers between devices with their start and end apart: 18, of which 8 were waited for; matrix products, arithmetic and copies ran while one was open for 5% of the time, Pallas kernels for 10%

profile of v1, /device:TPU:6, one launch (start us, length us, event | category | flops | bytes accessed | tf_op | source)
XLA Modules:
  0.0 106.7 jit_solution(1520814066812280219)
XLA Ops:
  0.0 1.1 slice_bitcast_fusion.18
  1.1 0.7 concatenate.6.place_ref
  1.8 0.0 copy-start
  1.8 2.2 %copy-done = bf16[1,32,256,256]{3,2,1,0:T(8,128)(2,1)S(1)} copy-done((bf16[1,32,256,256]{3,2,1,0:T(8,128)(2,1)S(1)}, bf16[1,32,256,256]{3,2,1,0:T(8,128)(2,1)}, u32[]{:S(2)}) %copy-start) | copy-done | bytes 4194328
  4.0 2.2 %copy-done.2 = bf16[1,32,256,256]{3,2,1,0:T(8,128)(2,1)S(1)} copy-done((bf16[1,32,256,256]{3,2,1,0:T(8,128)(2,1)S(1)}, bf16[1,32,256,256]{3,2,1,0:T(8,128)(2,1)}, u32[]{:S(2)}) %copy-start.2) | copy-done | bytes 4194328
  6.2 5.2 %shard_map.46 = (bf16[128,32,256]{2,1,0:T(8,128)(2,1)S(1)}, bf16[128,32,256]{2,1,0:T(8,128)(2,1)S(1)}) custom-call(s32[36]{0:T(128)S(1)} %concatenate.6.place_ref, bf16[256,256]{1,0:T(8,128)(2,1)S(1)} %get-tuple-element.29.psi_ref, bf16[32,256,256]{2,1,0:T(8,128)(2,1)S(1)} %bitcast.93, bf16[32,256,256]{2,1,0:T(8,128)(2,1)S(1)} %bitcast.96), custom_call_target="tpu_custom_call" | custom-call | flops 2147483648 | bytes 13631488 | tf_op jit(solution)/shard_map/pallas_call | solution.py:90
  11.4 0.1 collective-permute-start
  11.5 0.0 copy-start.1
  11.5 5.3 %shard_map.47 = (bf16[128,32,256]{2,1,0:T(8,128)(2,1)S(1)}, bf16[128,32,256]{2,1,0:T(8,128)(2,1)S(1)}) custom-call(s32[36]{0:T(128)S(1)} %concatenate.6.place_ref, bf16[256,256]{1,0:T(8,128)(2,1)S(1)} %get-tuple-element.31.psi_ref, bf16[32,256,256]{2,1,0:T(8,128)(2,1)S(1)} %bitcast.94, bf16[32,256,256]{2,1,0:T(8,128)(2,1)S(1)} %bitcast.97), custom_call_target="tpu_custom_call" | custom-call | flops 2147483648 | bytes 13631488 | tf_op jit(solution)/shard_map/pallas_call | solution.py:90
  16.8 0.6 collective-permute-start.4
  17.4 0.0 copy-done.1
  17.4 5.2 %shard_map.48 = (bf16[128,32,256]{2,1,0:T(8,128)(2,1)S(1)}, bf16[128,32,256]{2,1,0:T(8,128)(2,1)S(1)}) custom-call(s32[36]{0:T(128)S(1)} %concatenate.6.place_ref, bf16[256,256]{1,0:T(8,128)(2,1)S(1)} %get-tuple-element.30.psi_ref, bf16[32,256,256]{2,1,0:T(8,128)(2,1)S(1)} %bitcast.95, bf16[32,256,256]{2,1,0:T(8,128)(2,1)S(1)} %bitcast.98), custom_call_target="tpu_custom_call" | custom-call | flops 2147483648 | bytes 13631488 | tf_op jit(solution)/shard_map/pallas_call | solution.py:90
  22.7 0.1 collective-permute-start.10
  22.8 0.0 collective-permute-done
  22.8 0.4 add_convert_fusion.2
  23.2 2.0 %collective-permute-start.1 = (bf16[4,4,4,32,256]{4,3,2,1,0:T(8,128)(2,1)S(1)}, bf16[4,4,4,32,256]{4,3,2,1,0:T(8,128)(2,1)S(1)}, u32[]{:S(2)}, u32[]{:S(2)}) collective-permute-start(bf16[4,4,4,32,256]{4,3,2,1,0:T(8,128)(2,1)S(1)} %bitcast.106), channel_id=1, source_target_pairs={{0,4},{1,5},{2,6},{3,7},{4,0},{5,1},{6,2},{7,3},{8,12},{9,13},{10,... | collective-permute-start | bytes 3145736 | tf_op jit(solution)/shard_map/ppermute | solution.py:133
  25.2 0.0 collective-permute-done.4
  25.2 0.4 add_convert_fusion.1
  25.6 0.9 collective-permute-start.5
  26.5 0.4 collective-permute-done.10
  26.9 0.4 add_convert_fusion
  27.3 1.7 %collective-permute-start.11 = (bf16[2,4,8,32,256]{4,3,2,1,0:T(8,128)(2,1)S(1)}, bf16[2,4,8,32,256]{4,3,2,1,0:T(8,128)(2,1)S(1)}, u32[]{:S(2)}, u32[]{:S(2)}) collective-permute-start(bf16[2,4,8,32,256]{4,3,2,1,0:T(8,128)(2,1)S(1)} %bitcast.108), channel_id=1, source_target_pairs={{0,64},{1,65},{2,66},{3,67},{4,68},{5,69},{6,70},{7,71},{8,72},{9,... | collective-permute-start | bytes 3145736 | tf_op jit(solution)/shard_map/ppermute | solution.py:119
  29.0 0.4 convert_add_fusion.6
  29.4 0.2 convert_add_fusion.8
  29.6 0.2 convert_add_fusion.13
  29.7 0.4 convert_add_fusion.4
  30.2 7.9 %collective-permute-done.1 = bf16[4,4,4,32,256]{4,3,2,1,0:T(8,128)(2,1)S(1)} collective-permute-done((bf16[4,4,4,32,256]{4,3,2,1,0:T(8,128)(2,1)S(1)}, bf16[4,4,4,32,256]{4,3,2,1,0:T(8,128)(2,1)S(1)}, u32[]{:S(2)}, u32[]{:S(2)}) %collective-permute-start.1) | collective-permute-done | bytes 1048608 | tf_op jit(solution)/shard_map/ppermute | solution.py:133
  38.1 0.2 add_convert_fusion.3
  38.3 3.4 %collective-permute-start.2 = (bf16[2,4,4,32,256]{4,3,2,1,0:T(8,128)(2,1)S(1)}, bf16[2,4,4,32,256]{4,3,2,1,0:T(8,128)(2,1)S(1)}, u32[]{:S(2)}, u32[]{:S(2)}) collective-permute-start(bf16[2,4,4,32,256]{4,3,2,1,0:T(8,128)(2,1)S(1)} %add_convert_fusion.3), channel_id=1, source_target_pairs={{0,8},{1,9},{2,10},{3,11},{4,12},{5,13},{6,14},{7,15},{8,0},{9,1},... | collective-permute-start | bytes 1572872 | tf_op jit(solution)/shard_map/ppermute | solution.py:133
  41.6 0.0 collective-permute-done.5
  41.6 0.2 fusion.3
  41.9 0.6 collective-permute-start.6
  42.4 0.0 collective-permute-done.11
  42.4 0.2 fusion
  42.6 3.1 %collective-permute-start.12 = (bf16[4,8,32,256]{3,2,1,0:T(8,128)(2,1)S(1)}, bf16[4,8,32,256]{3,2,1,0:T(8,128)(2,1)S(1)}, u32[]{:S(2)}, u32[]{:S(2)}) collective-permute-start(bf16[4,8,32,256]{3,2,1,0:T(8,128)(2,1)S(1)} %fusion), channel_id=1, source_target_pairs={{0,192},{1,193},{2,194},{3,195},{4,196},{5,197},{6,198},{7,199},{8... | collective-permute-start | bytes 1572872 | tf_op jit(solution)/shard_map/ppermute | solution.py:119
  45.7 16.1 %collective-permute-done.2 = bf16[2,4,4,32,256]{4,3,2,1,0:T(8,128)(2,1)S(1)} collective-permute-done((bf16[2,4,4,32,256]{4,3,2,1,0:T(8,128)(2,1)S(1)}, bf16[2,4,4,32,256]{4,3,2,1,0:T(8,128)(2,1)S(1)}, u32[]{:S(2)}, u32[]{:S(2)}) %collective-permute-start.2) | collective-permute-done | bytes 524320 | tf_op jit(solution)/shard_map/ppermute | solution.py:133
  61.9 0.1 fusion.6
  62.0 5.7 %collective-permute-start.3 = (bf16[4,4,32,256]{3,2,1,0:T(8,128)(2,1)S(1)}, bf16[4,4,32,256]{3,2,1,0:T(8,128)(2,1)S(1)}, u32[]{:S(2)}, u32[]{:S(2)}) collective-permute-start(bf16[4,4,32,256]{3,2,1,0:T(8,128)(2,1)S(1)} %fusion.6), channel_id=1, source_target_pairs={{0,24},{1,25},{2,26},{3,27},{4,28},{5,29},{6,30},{7,31},{8,16},{9,... | collective-permute-start | bytes 786440 | tf_op jit(solution)/shard_map/ppermute | solution.py:133
  67.7 0.0 collective-permute-done.6
  67.7 0.3 fusion.5
  68.0 1.7 %collective-permute-start.7 = (bf16[8,32,256]{2,1,0:T(8,128)(2,1)S(1)}, bf16[8,32,256]{2,1,0:T(8,128)(2,1)S(1)}, u32[]{:S(2)}, u32[]{:S(2)}) collective-permute-start(bf16[8,32,256]{2,1,0:T(8,128)(2,1)S(1)} %get-tuple-element.23), channel_id=1, source_target_pairs={{0,64},{1,65},{2,66},{3,67},{4,68},{5,69},{6,70},{7,71},{8,72},{9,... | collective-permute-start | bytes 393224 | tf_op jit(solution)/shard_map/ppermute | solution.py:125
  69.7 2.9 %collective-permute-start.8 = (bf16[8,32,256]{2,1,0:T(8,128)(2,1)S(1)}, bf16[8,32,256]{2,1,0:T(8,128)(2,1)S(1)}, u32[]{:S(2)}, u32[]{:S(2)}) collective-permute-start(bf16[8,32,256]{2,1,0:T(8,128)(2,1)S(1)} %get-tuple-element.25), channel_id=1, source_target_pairs={{0,128},{1,129},{2,130},{3,131},{4,132},{5,133},{6,134},{7,135},{8... | collective-permute-start | bytes 393224 | tf_op jit(solution)/shard_map/ppermute | solution.py:125
  72.6 0.2 collective-permute-start.9
  72.8 0.0 collective-permute-done.12
  72.8 0.3 fusion.2
  73.1 0.9 collective-permute-start.13
  74.0 0.2 collective-permute-done.7
  74.2 1.4 %collective-permute-start.14 = (bf16[8,32,256]{2,1,0:T(8,128)(2,1)S(1)}, bf16[8,32,256]{2,1,0:T(8,128)(2,1)S(1)}, u32[]{:S(2)}, u32[]{:S(2)}) collective-permute-start(bf16[8,32,256]{2,1,0:T(8,128)(2,1)S(1)} %get-tuple-element.28), channel_id=1, source_target_pairs={{0,2},{1,3},{2,0},{3,1},{4,6},{5,7},{6,4},{7,5},{8,10},{9,11},{10,... | collective-permute-start | bytes 393224 | tf_op jit(solution)/shard_map/ppermute | solution.py:124
  75.7 1.6 %collective-permute-done.8 = bf16[8,32,256]{2,1,0:T(8,128)(2,1)S(1)} collective-permute-done((bf16[8,32,256]{2,1,0:T(8,128)(2,1)S(1)}, bf16[8,32,256]{2,1,0:T(8,128)(2,1)S(1)}, u32[]{:S(2)}, u32[]{:S(2)}) %collective-permute-start.8) | collective-permute-done | bytes 131104 | tf_op jit(solution)/shard_map/ppermute | solution.py:125
  77.2 0.7 collective-permute-start.15
  77.9 0.8 collective-permute-done.9
  78.7 0.1 fusion.15
  78.8 0.0 collective-permute-done.3
  78.8 0.9 fusion.8
  79.7 6.1 %all-to-all-start = ((bf16[16,32,256]{2,1,0:T(8,128)(2,1)}), bf16[16,32,256]{2,1,0:T(8,128)(2,1)S(1)}, u32[]{:S(2)}, u32[]{:S(2)}) async-start(bf16[16,32,256]{2,1,0:T(8,128)(2,1)} %bitcast.16), calls=%async_computation | async-start | bytes 524288 | tf_op jit(solution)/shard_map/all_to_all | solution.py:184
  85.8 0.0 collective-permute-done.13
  85.8 0.0 collective-permute-done.14
  85.9 0.0 collective-permute-done.15
  85.9 0.1 fusion.16
  85.9 0.7 pad_maximum_fusion
  86.7 5.5 %all-to-all-done = bf16[16,32,256]{2,1,0:T(8,128)(2,1)S(1)} async-done(((bf16[16,32,256]{2,1,0:T(8,128)(2,1)}), bf16[16,32,256]{2,1,0:T(8,128)(2,1)S(1)}, u32[]{:S(2)}, u32[]{:S(2)}) %all-to-all-start) | async-done | bytes 262176 | tf_op jit(solution)/shard_map/all_to_all | solution.py:184
  92.2 3.4 %all-to-all-start.1 = ((bf16[8,2,32,256]{3,2,1,0:T(8,128)(2,1)}), bf16[8,2,32,256]{3,2,1,0:T(8,128)(2,1)S(1)}, u32[]{:S(2)}, u32[]{:S(2)}) async-start(bf16[8,2,32,256]{3,2,1,0:T(8,128)(2,1)} %pad_maximum_fusion), calls=%async_computation.1 | async-start | bytes 524288 | tf_op jit(solution)/shard_map/all_to_all | solution.py:187
  95.6 10.4 %all-to-all-done.1 = bf16[8,2,32,256]{3,2,1,0:T(8,128)(2,1)S(1)} async-done(((bf16[8,2,32,256]{3,2,1,0:T(8,128)(2,1)}), bf16[8,2,32,256]{3,2,1,0:T(8,128)(2,1)S(1)}, u32[]{:S(2)}, u32[]{:S(2)}) %all-to-all-start.1) | async-done | bytes 262176 | tf_op jit(solution)/shard_map/all_to_all | solution.py:187
  106.0 0.6 maximum_bitcast_fusion
  (5 shorter events, 0.1 us)
Async XLA Ops:
  1.8 2.2 %copy-start = (bf16[1,32,256,256]{3,2,1,0:T(8,128)(2,1)S(1)}, bf16[1,32,256,256]{3,2,1,0:T(8,128)(2,1)}, u32[]{:S(2)}) copy-start(bf16[1,32,256,256]{3,2,1,0:T(8,128)(2,1)} %param.5) | copy-start | bytes 12582916
  4.0 2.2 %copy-start.2 = (bf16[1,32,256,256]{3,2,1,0:T(8,128)(2,1)S(1)}, bf16[1,32,256,256]{3,2,1,0:T(8,128)(2,1)}, u32[]{:S(2)}) copy-start(bf16[1,32,256,256]{3,2,1,0:T(8,128)(2,1)} %param.6) | copy-start | bytes 12582916
  11.4 11.3 %collective-permute-start = (bf16[128,32,256]{2,1,0:T(8,128)(2,1)S(1)}, bf16[128,32,256]{2,1,0:T(8,128)(2,1)S(1)}, u32[]{:S(2)}, u32[]{:S(2)}) collective-permute-start(bf16[128,32,256]{2,1,0:T(8,128)(2,1)S(1)} %get-tuple-element.12), channel_id=1, source_target_pairs={{0,32},{1,33},{2,34},{3,35},{4,36},{5,37},{6,38},{7,39},{8,40},{9,... | collective-permute-start | bytes 6291464 | tf_op jit(solution)/shard_map/ppermute | solution.py:113
  11.5 5.9 %copy-start.1 = (bf16[1,32,256,256]{3,2,1,0:T(8,128)(2,1)S(1)}, bf16[1,32,256,256]{3,2,1,0:T(8,128)(2,1)}, u32[]{:S(2)}) copy-start(bf16[1,32,256,256]{3,2,1,0:T(8,128)(2,1)} %param.5) | copy-start | bytes 12582916
  16.8 8.4 %collective-permute-start.4 = (bf16[128,32,256]{2,1,0:T(8,128)(2,1)S(1)}, bf16[128,32,256]{2,1,0:T(8,128)(2,1)S(1)}, u32[]{:S(2)}, u32[]{:S(2)}) collective-permute-start(bf16[128,32,256]{2,1,0:T(8,128)(2,1)S(1)} %get-tuple-element.14), channel_id=1, source_target_pairs={{0,32},{1,33},{2,34},{3,35},{4,36},{5,37},{6,38},{7,39},{8,40},{9,... | collective-permute-start | bytes 6291464 | tf_op jit(solution)/shard_map/ppermute | solution.py:113
  22.7 4.2 %collective-permute-start.10 = (bf16[128,32,256]{2,1,0:T(8,128)(2,1)S(1)}, bf16[128,32,256]{2,1,0:T(8,128)(2,1)S(1)}, u32[]{:S(2)}, u32[]{:S(2)}) collective-permute-start(bf16[128,32,256]{2,1,0:T(8,128)(2,1)S(1)} %get-tuple-element.16), channel_id=1, source_target_pairs={{0,32},{1,33},{2,34},{3,35},{4,36},{5,37},{6,38},{7,39},{8,40},{9,... | collective-permute-start | bytes 6291464 | tf_op jit(solution)/shard_map/ppermute | solution.py:113
  23.2 14.9 %collective-permute-start.1 = (bf16[4,4,4,32,256]{4,3,2,1,0:T(8,128)(2,1)S(1)}, bf16[4,4,4,32,256]{4,3,2,1,0:T(8,128)(2,1)S(1)}, u32[]{:S(2)}, u32[]{:S(2)}) collective-permute-start(bf16[4,4,4,32,256]{4,3,2,1,0:T(8,128)(2,1)S(1)} %bitcast.106), channel_id=1, source_target_pairs={{0,4},{1,5},{2,6},{3,7},{4,0},{5,1},{6,2},{7,3},{8,12},{9,13},{10,... | collective-permute-start | bytes 3145736 | tf_op jit(solution)/shard_map/ppermute | solution.py:133
  25.6 16.0 %collective-permute-start.5 = (bf16[2,4,8,32,256]{4,3,2,1,0:T(8,128)(2,1)S(1)}, bf16[2,4,8,32,256]{4,3,2,1,0:T(8,128)(2,1)S(1)}, u32[]{:S(2)}, u32[]{:S(2)}) collective-permute-start(bf16[2,4,8,32,256]{4,3,2,1,0:T(8,128)(2,1)S(1)} %bitcast.107), channel_id=1, source_target_pairs={{0,1},{1,0},{2,3},{3,2},{4,5},{5,4},{6,7},{7,6},{8,9},{9,8},{10,11... | collective-permute-start | bytes 3145736 | tf_op jit(solution)/shard_map/ppermute | solution.py:118
  27.3 15.1 %collective-permute-start.11 = (bf16[2,4,8,32,256]{4,3,2,1,0:T(8,128)(2,1)S(1)}, bf16[2,4,8,32,256]{4,3,2,1,0:T(8,128)(2,1)S(1)}, u32[]{:S(2)}, u32[]{:S(2)}) collective-permute-start(bf16[2,4,8,32,256]{4,3,2,1,0:T(8,128)(2,1)S(1)} %bitcast.108), channel_id=1, source_target_pairs={{0,64},{1,65},{2,66},{3,67},{4,68},{5,69},{6,70},{7,71},{8,72},{9,... | collective-permute-start | bytes 3145736 | tf_op jit(solution)/shard_map/ppermute | solution.py:119
  38.3 23.6 %collective-permute-start.2 = (bf16[2,4,4,32,256]{4,3,2,1,0:T(8,128)(2,1)S(1)}, bf16[2,4,4,32,256]{4,3,2,1,0:T(8,128)(2,1)S(1)}, u32[]{:S(2)}, u32[]{:S(2)}) collective-permute-start(bf16[2,4,4,32,256]{4,3,2,1,0:T(8,128)(2,1)S(1)} %add_convert_fusion.3), channel_id=1, source_target_pairs={{0,8},{1,9},{2,10},{3,11},{4,12},{5,13},{6,14},{7,15},{8,0},{9,1},... | collective-permute-start | bytes 1572872 | tf_op jit(solution)/shard_map/ppermute | solution.py:133
  41.9 25.8 %collective-permute-start.6 = (bf16[4,8,32,256]{3,2,1,0:T(8,128)(2,1)S(1)}, bf16[4,8,32,256]{3,2,1,0:T(8,128)(2,1)S(1)}, u32[]{:S(2)}, u32[]{:S(2)}) collective-permute-start(bf16[4,8,32,256]{3,2,1,0:T(8,128)(2,1)S(1)} %fusion.3), channel_id=1, source_target_pairs={{0,3},{1,2},{2,1},{3,0},{4,7},{5,6},{6,5},{7,4},{8,11},{9,10},{10,... | collective-permute-start | bytes 1572872 | tf_op jit(solution)/shard_map/ppermute | solution.py:118
  42.6 30.2 %collective-permute-start.12 = (bf16[4,8,32,256]{3,2,1,0:T(8,128)(2,1)S(1)}, bf16[4,8,32,256]{3,2,1,0:T(8,128)(2,1)S(1)}, u32[]{:S(2)}, u32[]{:S(2)}) collective-permute-start(bf16[4,8,32,256]{3,2,1,0:T(8,128)(2,1)S(1)} %fusion), channel_id=1, source_target_pairs={{0,192},{1,193},{2,194},{3,195},{4,196},{5,197},{6,198},{7,199},{8... | collective-permute-start | bytes 1572872 | tf_op jit(solution)/shard_map/ppermute | solution.py:119
  62.0 16.8 %collective-permute-start.3 = (bf16[4,4,32,256]{3,2,1,0:T(8,128)(2,1)S(1)}, bf16[4,4,32,256]{3,2,1,0:T(8,128)(2,1)S(1)}, u32[]{:S(2)}, u32[]{:S(2)}) collective-permute-start(bf16[4,4,32,256]{3,2,1,0:T(8,128)(2,1)S(1)} %fusion.6), channel_id=1, source_target_pairs={{0,24},{1,25},{2,26},{3,27},{4,28},{5,29},{6,30},{7,31},{8,16},{9,... | collective-permute-start | bytes 786440 | tf_op jit(solution)/shard_map/ppermute | solution.py:133
  68.0 6.2 %collective-permute-start.7 = (bf16[8,32,256]{2,1,0:T(8,128)(2,1)S(1)}, bf16[8,32,256]{2,1,0:T(8,128)(2,1)S(1)}, u32[]{:S(2)}, u32[]{:S(2)}) collective-permute-start(bf16[8,32,256]{2,1,0:T(8,128)(2,1)S(1)} %get-tuple-element.23), channel_id=1, source_target_pairs={{0,64},{1,65},{2,66},{3,67},{4,68},{5,69},{6,70},{7,71},{8,72},{9,... | collective-permute-start | bytes 393224 | tf_op jit(solution)/shard_map/ppermute | solution.py:125
  69.7 7.6 %collective-permute-start.8 = (bf16[8,32,256]{2,1,0:T(8,128)(2,1)S(1)}, bf16[8,32,256]{2,1,0:T(8,128)(2,1)S(1)}, u32[]{:S(2)}, u32[]{:S(2)}) collective-permute-start(bf16[8,32,256]{2,1,0:T(8,128)(2,1)S(1)} %get-tuple-element.25), channel_id=1, source_target_pairs={{0,128},{1,129},{2,130},{3,131},{4,132},{5,133},{6,134},{7,135},{8... | collective-permute-start | bytes 393224 | tf_op jit(solution)/shard_map/ppermute | solution.py:125
  72.6 6.2 %collective-permute-start.9 = (bf16[8,32,256]{2,1,0:T(8,128)(2,1)S(1)}, bf16[8,32,256]{2,1,0:T(8,128)(2,1)S(1)}, u32[]{:S(2)}, u32[]{:S(2)}) collective-permute-start(bf16[8,32,256]{2,1,0:T(8,128)(2,1)S(1)} %get-tuple-element.24), channel_id=1, source_target_pairs={{0,192},{1,193},{2,194},{3,195},{4,196},{5,197},{6,198},{7,199},{8... | collective-permute-start | bytes 393224 | tf_op jit(solution)/shard_map/ppermute | solution.py:125
  73.1 12.7 %collective-permute-start.13 = (bf16[8,32,256]{2,1,0:T(8,128)(2,1)S(1)}, bf16[8,32,256]{2,1,0:T(8,128)(2,1)S(1)}, u32[]{:S(2)}, u32[]{:S(2)}) collective-permute-start(bf16[8,32,256]{2,1,0:T(8,128)(2,1)S(1)} %get-tuple-element.26), channel_id=1, source_target_pairs={{0,1},{1,0},{2,3},{3,2},{4,5},{5,4},{6,7},{7,6},{8,9},{9,8},{10,11... | collective-permute-start | bytes 393224 | tf_op jit(solution)/shard_map/ppermute | solution.py:124
  74.2 11.6 %collective-permute-start.14 = (bf16[8,32,256]{2,1,0:T(8,128)(2,1)S(1)}, bf16[8,32,256]{2,1,0:T(8,128)(2,1)S(1)}, u32[]{:S(2)}, u32[]{:S(2)}) collective-permute-start(bf16[8,32,256]{2,1,0:T(8,128)(2,1)S(1)} %get-tuple-element.28), channel_id=1, source_target_pairs={{0,2},{1,3},{2,0},{3,1},{4,6},{5,7},{6,4},{7,5},{8,10},{9,11},{10,... | collective-permute-start | bytes 393224 | tf_op jit(solution)/shard_map/ppermute | solution.py:124
  77.2 8.6 %collective-permute-start.15 = (bf16[8,32,256]{2,1,0:T(8,128)(2,1)S(1)}, bf16[8,32,256]{2,1,0:T(8,128)(2,1)S(1)}, u32[]{:S(2)}, u32[]{:S(2)}) collective-permute-start(bf16[8,32,256]{2,1,0:T(8,128)(2,1)S(1)} %get-tuple-element.27), channel_id=1, source_target_pairs={{0,3},{1,2},{2,1},{3,0},{4,7},{5,6},{6,5},{7,4},{8,11},{9,10},{10,... | collective-permute-start | bytes 393224 | tf_op jit(solution)/shard_map/ppermute | solution.py:124
  79.7 12.5 %all-to-all-start = ((bf16[16,32,256]{2,1,0:T(8,128)(2,1)}), bf16[16,32,256]{2,1,0:T(8,128)(2,1)S(1)}, u32[]{:S(2)}, u32[]{:S(2)}) async-start(bf16[16,32,256]{2,1,0:T(8,128)(2,1)} %bitcast.16), calls=%async_computation | async-start | bytes 524288 | tf_op jit(solution)/shard_map/all_to_all | solution.py:184
  92.2 13.8 %all-to-all-start.1 = ((bf16[8,2,32,256]{3,2,1,0:T(8,128)(2,1)}), bf16[8,2,32,256]{3,2,1,0:T(8,128)(2,1)S(1)}, u32[]{:S(2)}, u32[]{:S(2)}) async-start(bf16[8,2,32,256]{3,2,1,0:T(8,128)(2,1)} %pad_maximum_fusion), calls=%async_computation.1 | async-start | bytes 524288 | tf_op jit(solution)/shard_map/all_to_all | solution.py:187

commit v2 on v0

v2 whole, which is shorter than its diff:
```python
import functools

import jax
import jax.numpy as jnp
import numpy as np
from jax import lax
from jax.experimental import pallas as pl
from jax.experimental.pallas import tpu as pltpu
from jax.sharding import Mesh, PartitionSpec as P

AXES = ("y", "c", "z", "x")
SIZES = (4, 2, 8, 4)
K = 256
TERMS = 32
ROWS = 32
CHUNKS = (4, 4, 8, 16)
LATER_CHUNKS = (16, 16)

VMEM = pl.BlockSpec(memory_space=pltpu.VMEM)
SMEM = pl.BlockSpec(memory_space=pltpu.SMEM)
HBM = pl.BlockSpec(memory_space=pltpu.HBM)
ANY = pl.BlockSpec(memory_space=pl.ANY)


def gray(n):
    return n ^ (n >> 1)


def ring_slot(distance, core):
    return gray(jnp.where(core == 0, (4 - distance) & 3, distance))


def ring_distance(slot, core):
    return jnp.where(core == 0, (4 - gray(slot)) & 3, gray(slot))


HALF = ROWS // 2
PARTS = 6


def layout(part, b_z, b_x, x, c):
    return ring_slot(b_x ^ x, c) * (32 if part % 2 == 0 else 8) + b_z


def row(part, j):
    return j * (8 if part % 2 == 0 else 32)


def add_products(vectors, first, n, target_ref, psi_ref, left_ref, right_ref, keeps, sends):
    y, c, x = (lax.axis_index(a) for a in ("y", "c", "x"))
    cores = (c, 1 - c)
    rows = [
        pl.multiple_of(((y ^ ring_distance(j, core)) * 2 + core) * ROWS, ROWS) for core in cores for j in range(4)
    ]
    left = jnp.concatenate([left_ref[0, first + t, pl.ds(r, ROWS), :] for t in range(n) for r in rows], axis=0)
    turned = [jnp.dot(left, psi_ref[0, v], preferred_element_type=jnp.float32).astype(jnp.bfloat16) for v in vectors]
    for t in range(n):
        product = lax.dot_general(
            jnp.concatenate([a[t * K:(t + 1) * K] for a in turned], axis=0),
            right_ref[0, first + t],
            (((1,), (1,)), ((), ())),
            preferred_element_type=jnp.float32,
        )
        target = target_ref[0, first + t, 0]
        for i in range(2 * len(vectors)):
            part = 2 * vectors[0] + i
            for other, ref in enumerate((keeps[i], sends[i])):
                base = layout(part, target >> 2, target & 3, x, cores[other])
                for j in range(4):
                    begin = i // 2 * K + (other * 4 + j) * ROWS + i % 2 * HALF
                    at = base + row(part, j)
                    ref[at] = (ref[at].astype(jnp.float32) + product[begin:begin + HALF]).astype(jnp.bfloat16)


def first_kernel(target_ref, psi_hbm, left_hbm, right_hbm, *refs):
    keeps, sends = refs[:2], refs[2:4]
    token_ref, psi_ref, left_ref, right_ref, sems = refs[4:]
    copies = [pltpu.make_async_copy(psi_hbm, psi_ref, sems.at[2, 0])]
    first = 0
    for i, n in enumerate(CHUNKS):
        at = pl.ds(first, n)
        copies.append(pltpu.make_async_copy(left_hbm.at[:, at], left_ref.at[:, at], sems.at[0, i]))
        copies.append(pltpu.make_async_copy(right_hbm.at[:, at], right_ref.at[:, at], sems.at[1, i]))
        first += n
    for copy in copies:
        copy.start()
    for ref in (*keeps, *sends, token_ref):
        ref[...] = jnp.zeros_like(ref)
    copies[0].wait()
    first = 0
    for i, n in enumerate(CHUNKS):
        copies[2 * i + 1].wait()
        copies[2 * i + 2].wait()
        add_products((0,), first, n, target_ref, psi_ref, left_ref, right_ref, keeps, sends)
        first += n


def later_kernel(vectors, after_ref, target_ref, psi_ref, left_ref, right_ref, *refs):
    n = 2 * len(vectors)
    keeps, sends, token_ref = refs[:n], refs[n:2 * n], refs[2 * n]
    for ref in (*keeps, *sends, token_ref):
        ref[...] = jnp.zeros_like(ref)
    first = 0
    for n in LATER_CHUNKS:
        add_products(vectors, first, n, target_ref, psi_ref, left_ref, right_ref, keeps, sends)
        first += n


def blocks(n):
    return jax.ShapeDtypeStruct((n, HALF, K), jnp.bfloat16)


TOKEN = jax.ShapeDtypeStruct((8, 128), jnp.float32)
LIMIT = pltpu.CompilerParams(vmem_limit_bytes=24 * 2**20)
SMALL = pl.CostEstimate(flops=1, bytes_accessed=1, transcendentals=0)


def first_products(target, *arrays):
    arrays = [pltpu.with_memory_space_constraint(a, pltpu.HBM) for a in arrays]
    return pl.pallas_call(
        first_kernel,
        in_specs=[SMEM, HBM, HBM, HBM],
        out_specs=[VMEM] * 8,
        out_shape=[blocks(128)] * 4 + [TOKEN] + [jax.ShapeDtypeStruct(a.shape, a.dtype) for a in arrays],
        scratch_shapes=[pltpu.SemaphoreType.DMA((3, len(CHUNKS)))],
        compiler_params=LIMIT,
        cost_estimate=SMALL,
        name="first_products",
    )(target, *arrays)


def later_products(token, vectors, target, *arrays):
    return pl.pallas_call(
        functools.partial(later_kernel, vectors),
        in_specs=[ANY, SMEM, VMEM, VMEM, VMEM],
        out_specs=[VMEM] * (4 * len(vectors) + 1),
        out_shape=[blocks(128)] * (4 * len(vectors)) + [TOKEN],
        compiler_params=LIMIT,
        cost_estimate=SMALL,
        name="later_products",
    )(token, target, *arrays)


def gather_arrays(sums):
    arrays, places = [], []
    for terms in sums:
        for a, _ in terms:
            if not any(a is b for b in arrays):
                arrays.append(a)
        places.append([(next(k for k, b in enumerate(arrays) if b is a), start) for a, start in terms])
    return arrays, places


def combine_kernel(n, places, *refs):
    ins, out, token_ref = refs[1:-2], refs[-2], refs[-1]
    token_ref[...] = jnp.zeros_like(token_ref)
    for s, terms in enumerate(places):

        @pl.loop(0, n, unroll=4)
        def _(i):
            value = sum(ins[k][start + i].astype(jnp.float32) for k, start in terms)
            out[s * n + i] = value.astype(jnp.bfloat16)


def combine(token, n, sums):
    arrays, places = gather_arrays(sums)
    return pl.pallas_call(
        functools.partial(combine_kernel, n, places),
        in_specs=[ANY] + [VMEM] * len(arrays),
        out_specs=[VMEM] * 2,
        out_shape=[blocks(n * len(sums)), TOKEN],
        compiler_params=LIMIT,
        cost_estimate=SMALL,
        name="combine",
    )(token, *arrays)


def permutation(move):
    pairs = []
    for index in range(256):
        place = [int(v) for v in np.unravel_index(index, SIZES)]
        pairs.append((index, int(np.ravel_multi_index(move(*place), SIZES))))
    return pairs


def distance_of(slot, core):
    return (4 - gray(slot)) & 3 if core == 0 else gray(slot)


def core_swap(a):
    return lax.ppermute(a, AXES, permutation(lambda y, c, z, x: (y, 1 - c, z, x)))


def swap(a, y_slot=0, x_slot=0):
    def move(y, c, z, x):
        return (y ^ distance_of(y_slot, c), c, z, x ^ distance_of(x_slot, c))

    return lax.ppermute(a, AXES, permutation(move))


def last_kernel(places, *refs):
    ins, out = refs[1:-1], refs[-1]

    @pl.loop(0, 8)
    def _(b):
        for part, terms in enumerate(places):
            value = sum(ins[k][start + b].astype(jnp.float32) for k, start in terms)
            out[b, part // 2, part % 2 * HALF:(part % 2 + 1) * HALF] = value.astype(jnp.bfloat16)


def last_sends(token, parts):
    arrays, places = gather_arrays(parts)
    return pl.pallas_call(
        functools.partial(last_kernel, places),
        in_specs=[ANY] + [VMEM] * len(arrays),
        out_specs=VMEM,
        out_shape=jax.ShapeDtypeStruct((8, PARTS // 2, ROWS, K), jnp.bfloat16),
        compiler_params=LIMIT,
        cost_estimate=SMALL,
        name="last_sends",
    )(token, *arrays)


ORDER = [
    (1, (0,)), (1, (1,)), (1, (2,)), (1, (3,)), (1, (4,)), (1, (5,)),
    (2, (0, 2)), (2, (1, 3)), (2, (4,)), (2, (5,)),
    (3, (0, 2)), (3, (1, 3)), (3, (4,)), (3, (5,)),
    (4, (0, 2, 4)), (4, (1, 3, 5)),
]


def body(wavefunction, left_operators, right_operators, target_sector):
    parts = []

    def start(sums):
        n = len(sums) // 2
        parts.extend([(sums[i], 0), (core_swap(sums[n + i]), 0)] for i in range(n))

    def run(token, order):
        for step, members in order:
            n = 128 >> step
            out, token = combine(token, n, [[(a, at + n) for a, at in parts[p]] for p in members])
            along_x = (members[0] % 2 == 0) == (step <= 2)
            got = swap(out, **{"x_slot" if along_x else "y_slot": 2 if step % 2 else 1})
            for i, p in enumerate(members):
                parts[p].append((got, i * n))
        return token

    *sums, token, psi, left, right = first_products(target_sector, wavefunction, left_operators, right_operators)
    start(sums)
    *sums, token = later_products(token, (1, 2), target_sector, psi, left, right)
    start(sums)
    token = run(token, ORDER)
    spread = lax.all_to_all(last_sends(token, parts), "z", 0, 0, tiled=True)
    return jnp.sum(spread.astype(jnp.float32), axis=0)[None]


def solution(mesh):
    fine = Mesh(np.array(mesh.devices).reshape(SIZES), AXES)
    return jax.shard_map(
        body,
        mesh=fine,
        in_specs=(
            P(("z", "x"), None, None, None),
            P(("z", "x"), ("y", "c"), None, None),
            P(("z", "x"), ("y", "c"), None, None),
            P(("z", "x"), ("y", "c"), None),
        ),
        out_specs=P(("z", "x"), None, ("y", "c"), None),
        check_vma=False,
    )
```

time: 714 us -> 85 us (0.12)
  blocking collectives: 556 us -> 20.3 us
  waiting for transfers between devices: 62.6 us -> 18 us
  other arithmetic: 44.5 us -> 0.7 us
  starting transfers between devices: 0.01 us -> 29.7 us
  matrix products: 20.9 us -> 0 us
  Pallas kernels: 0 us -> 15.2 us
  local copies, waits for them, and re-layouts: 15.6 us -> 0.74 us
  between operations: 13.4 us -> 0.18 us
    all_to_all x1, blocking collectives: 556 us -> 20.3 us  [body(): spread = lax.all_to_all(last_sends(token, parts), 'z', 0, 0, tiled=True)]
    psum x1 -> x0, waiting for transfers between devices: 62.6 us -> none  [body(): lax.psum(partial_value.astype(jnp.bfloat16), 'term').astype(jnp.float32)]
    reduce_sum x4 -> x1, other arithmetic: 30.5 us -> 0.7 us  [body(): return jnp.sum(spread.astype(jnp.float32), axis=0)[None]]
    ppermute x0 -> x22, starting transfers between devices: none -> 29.7 us  [the longest x16 28 us: swap(): return lax.ppermute(a, AXES, permutation(move))]
    dot_general x4 -> x0, matrix products: 20.9 us -> none  [one_batch(): jnp.einsum('qdk,qfks->qfds', left_factor, partial_contraction, preferred_...]
    ppermute x0 -> x22, waiting for transfers between devices: none -> 18 us  [the longest x16 17.7 us: swap(): return lax.ppermute(a, AXES, permutation(move))]
    pallas_call x0 -> x19, Pallas kernels: none -> 15.2 us  [the longest x1 6.28 us: later_products(): pl.pallas_call(functools.partial(later_kernel, vectors), in_specs=[ANY, S...]
    gather x1 -> x0, local copies, waits for them, and re-layouts: 14.8 us -> none  [body(): products[source]]
  transfers between devices with their start and end apart: 1 -> 22, of which waited for: 1 -> 11; matrix products, arithmetic and copies ran while one was open for 0% -> 0% of each run, Pallas kernels for 0% -> 11%
where the time goes in v2:
time: 85 us; the launch traced here: 84.8 us
  starting transfers between devices  29.7 us (35%)
  blocking collectives  20.3 us (24%)
  waiting for transfers between devices  18 us (21%)
  Pallas kernels  15.2 us (18%)
    ppermute x16, starting transfers between devices, swap(): return lax.ppermute(a, AXES, permutation(move))  28 us
    all_to_all x1, blocking collectives, body(): spread = lax.all_to_all(last_sends(token, parts), 'z', 0, 0, tiled=True)  20.3 us
    ppermute x16, waiting for transfers between devices, swap(): return lax.ppermute(a, AXES, permutation(move))  17.7 us
    pallas_call x1, Pallas kernels, later_products(): pl.pallas_call(functools.partial(later_kernel, vectors), in_specs=[ANY, S...  6.28 us
    pallas_call x1, Pallas kernels, first_products(): pl.pallas_call(first_kernel, in_specs=[SMEM, HBM, HBM, HBM], out_specs=[V...  5.94 us
    pallas_call x16, Pallas kernels, combine(): pl.pallas_call(functools.partial(combine_kernel, n, places), in_specs=[AN...  2.67 us
  transfers between devices with their start and end apart: 22, of which 11 were waited for; matrix products, arithmetic and copies ran while one was open for 0% of the time, Pallas kernels for 11%

profile of v2, /device:TPU:6, one launch (start us, length us, event | category | flops | bytes accessed | tf_op | source)
XLA Modules:
  0.0 84.8 jit_solution(6736195360521971275)
XLA Ops:
  0.0 0.7 copy.5.target_ref
  0.7 5.9 %first_products.1 = (bf16[128,16,256]{2,1,0:T(8,128)(2,1)S(1)}, bf16[128,16,256]{2,1,0:T(8,128)(2,1)S(1)}, bf16[128,16,256]{2,1,0:T(8,128)(2,1)S(1)}, bf16[128,1...) custom-call(s32[1,32,1]{2,1,0:T(8,128)S(1)} %copy.5.target_ref, ...), custom_call_target="tpu_custom_call" | custom-call | flops 1 | bytes 1 | tf_op jit(solution)/shard_map/first_products/pallas_call | solution.py:120
  6.7 0.1 collective-permute-start
  6.8 0.5 collective-permute-start.1
  7.3 6.3 %later_products.1 = (bf16[128,16,256]{2,1,0:T(8,128)(2,1)S(1)}, bf16[128,16,256]{2,1,0:T(8,128)(2,1)S(1)}, bf16[128,16,256]{2,1,0:T(8,128)(2,1)S(1)}, bf16[128,1...) custom-call(f32[8,128]{1,0:T(8,128)S(1)} %get-tuple-element.54.after, ...), custom_call_target="tpu_custom_call" | custom-call | flops 1 | bytes 1 | tf_op jit(solution)/shard_map/later_products/pallas_call | solution.py:133
  13.6 0.2 collective-permute-start.2
  13.7 0.4 collective-permute-start.3
  14.2 0.1 collective-permute-start.4
  14.3 0.0 collective-permute-done.refs_2_
  14.3 0.4 collective-permute-start.5
  14.7 0.2 combine.16
  14.9 0.0 collective-permute-done.1.refs_2_.refs_8_
  14.9 1.1 %collective-permute-start.6 = (bf16[64,16,256]{2,1,0:T(8,128)(2,1)S(1)}, bf16[64,16,256]{2,1,0:T(8,128)(2,1)S(1)}, u32[]{:S(2)}, u32[]{:S(2)}) collective-permute-start(bf16[64,16,256]{2,1,0:T(8,128)(2,1)S(1)} %get-tuple-element.77), channel_id=1, source_target_pairs={{0,1},{1,0},{2,3},{3,2},{4,5},{5,4},{6,7},{7,6},{8,9},{9,8},{10,11... | collective-permute-start | bytes 1572872 | tf_op jit(solution)/shard_map/ppermute | solution.py:198
  16.0 0.2 combine.17
  16.2 0.2 collective-permute-done.2.refs_2_.refs_5_.refs_6_.refs_7_.refs_14_
  16.3 0.2 combine.18
  16.5 1.2 %collective-permute-start.7 = (bf16[64,16,256]{2,1,0:T(8,128)(2,1)S(1)}, bf16[64,16,256]{2,1,0:T(8,128)(2,1)S(1)}, u32[]{:S(2)}, u32[]{:S(2)}) collective-permute-start(bf16[64,16,256]{2,1,0:T(8,128)(2,1)S(1)} %get-tuple-element.78), channel_id=1, source_target_pairs={{0,1},{1,0},{2,3},{3,2},{4,5},{5,4},{6,7},{7,6},{8,9},{9,8},{10,11... | collective-permute-start | bytes 1572872 | tf_op jit(solution)/shard_map/ppermute | solution.py:198
  17.7 0.2 collective-permute-done.3.refs_2_.refs_5_.refs_6_.refs_7_.refs_17_
  17.8 0.2 combine.19
  18.0 1.7 %collective-permute-start.9 = (bf16[64,16,256]{2,1,0:T(8,128)(2,1)S(1)}, bf16[64,16,256]{2,1,0:T(8,128)(2,1)S(1)}, u32[]{:S(2)}, u32[]{:S(2)}) collective-permute-start(bf16[64,16,256]{2,1,0:T(8,128)(2,1)S(1)} %get-tuple-element.81), channel_id=1, source_target_pairs={{0,64},{1,65},{2,66},{3,67},{4,68},{5,69},{6,70},{7,71},{8,72},{9,... | collective-permute-start | bytes 1572872 | tf_op jit(solution)/shard_map/ppermute | solution.py:198
  19.7 0.0 collective-permute-done.4.refs_2_.refs_10_.refs_20_
  19.7 1.2 %collective-permute-start.8 = (bf16[64,16,256]{2,1,0:T(8,128)(2,1)S(1)}, bf16[64,16,256]{2,1,0:T(8,128)(2,1)S(1)}, u32[]{:S(2)}, u32[]{:S(2)}) collective-permute-start(bf16[64,16,256]{2,1,0:T(8,128)(2,1)S(1)} %get-tuple-element.80), channel_id=1, source_target_pairs={{0,64},{1,65},{2,66},{3,67},{4,68},{5,69},{6,70},{7,71},{8,72},{9,... | collective-permute-start | bytes 1572872 | tf_op jit(solution)/shard_map/ppermute | solution.py:198
  20.9 0.2 combine.20
  21.1 0.0 collective-permute-done.5.refs_2_.refs_10_.refs_25_
  21.1 0.9 %collective-permute-start.10 = (bf16[64,16,256]{2,1,0:T(8,128)(2,1)S(1)}, bf16[64,16,256]{2,1,0:T(8,128)(2,1)S(1)}, u32[]{:S(2)}, u32[]{:S(2)}) collective-permute-start(bf16[64,16,256]{2,1,0:T(8,128)(2,1)S(1)} %get-tuple-element.83), channel_id=1, source_target_pairs={{0,1},{1,0},{2,3},{3,2},{4,5},{5,4},{6,7},{7,6},{8,9},{9,8},{10,11... | collective-permute-start | bytes 1572872 | tf_op jit(solution)/shard_map/ppermute | solution.py:198
  22.0 0.2 combine.21
  22.2 2.1 %collective-permute-done.6.refs_3_ = bf16[64,16,256]{2,1,0:T(8,128)(2,1)S(1)} collective-permute-done((bf16[64,16,256]{2,1,0:T(8,128)(2,1)S(1)}, bf16[64,16,256]{2,1,0:T(8,128)(2,1)S(1)}, u32[]{:S(2)}, u32[]{:S(2)}) %collective-permute-start.6) | collective-permute-done | bytes 524320 | tf_op jit(solution)/shard_map/ppermute | solution.py:198
  24.3 1.6 %collective-permute-start.11 = (bf16[64,16,256]{2,1,0:T(8,128)(2,1)S(1)}, bf16[64,16,256]{2,1,0:T(8,128)(2,1)S(1)}, u32[]{:S(2)}, u32[]{:S(2)}) collective-permute-start(bf16[64,16,256]{2,1,0:T(8,128)(2,1)S(1)} %get-tuple-element.85), channel_id=1, source_target_pairs={{0,64},{1,65},{2,66},{3,67},{4,68},{5,69},{6,70},{7,71},{8,72},{9,... | collective-permute-start | bytes 1572872 | tf_op jit(solution)/shard_map/ppermute | solution.py:198
  25.9 4.0 %collective-permute-done.7.refs_6_.refs_7_.refs_8_.refs_15_ = bf16[64,16,256]{2,1,0:T(8,128)(2,1)S(1)} collective-permute-done((bf16[64,16,256]{2,1,0:T(8,128)(2,1)S(1)}, bf16[64,16,256]{2,1,0:T(8,128)(2,1)S(1)}, u32[]{:S(2)}, u32[]{:S(2)}) %collective-permute-start.7) | collective-permute-done | bytes 524320 | tf_op jit(solution)/shard_map/ppermute | solution.py:198
  29.9 0.3 combine.22
  30.2 2.3 %collective-permute-start.12 = (bf16[64,16,256]{2,1,0:T(8,128)(2,1)S(1)}, bf16[64,16,256]{2,1,0:T(8,128)(2,1)S(1)}, u32[]{:S(2)}, u32[]{:S(2)}) collective-permute-start(bf16[64,16,256]{2,1,0:T(8,128)(2,1)S(1)} %get-tuple-element.87), channel_id=1, source_target_pairs={{0,3},{1,2},{2,1},{3,0},{4,7},{5,6},{6,5},{7,4},{8,11},{9,10},{10,... | collective-permute-start | bytes 1572872 | tf_op jit(solution)/shard_map/ppermute | solution.py:198
  32.5 0.4 collective-permute-done.8.refs_3_.refs_9_
  32.9 0.3 combine.23
  33.2 3.1 %collective-permute-start.13 = (bf16[64,16,256]{2,1,0:T(8,128)(2,1)S(1)}, bf16[64,16,256]{2,1,0:T(8,128)(2,1)S(1)}, u32[]{:S(2)}, u32[]{:S(2)}) collective-permute-start(bf16[64,16,256]{2,1,0:T(8,128)(2,1)S(1)} %get-tuple-element.89), channel_id=1, source_target_pairs={{0,192},{1,193},{2,194},{3,195},{4,196},{5,197},{6,198},{7,199},{8... | collective-permute-start | bytes 1572872 | tf_op jit(solution)/shard_map/ppermute | solution.py:198
  36.3 1.7 %collective-permute-done.10.refs_3_.refs_11_.refs_21_ = bf16[64,16,256]{2,1,0:T(8,128)(2,1)S(1)} collective-permute-done((bf16[64,16,256]{2,1,0:T(8,128)(2,1)S(1)}, bf16[64,16,256]{2,1,0:T(8,128)(2,1)S(1)}, u32[]{:S(2)}, u32[]{:S(2)}) %collective-permute-start.10) | collective-permute-done | bytes 524320 | tf_op jit(solution)/shard_map/ppermute | solution.py:198
  38.0 0.1 combine.24
  38.1 2.3 %collective-permute-start.14 = (bf16[32,16,256]{2,1,0:T(8,128)(2,1)S(1)}, bf16[32,16,256]{2,1,0:T(8,128)(2,1)S(1)}, u32[]{:S(2)}, u32[]{:S(2)}) collective-permute-start(bf16[32,16,256]{2,1,0:T(8,128)(2,1)S(1)} %get-tuple-element.91), channel_id=1, source_target_pairs={{0,3},{1,2},{2,1},{3,0},{4,7},{5,6},{6,5},{7,4},{8,11},{9,10},{10,... | collective-permute-start | bytes 786440 | tf_op jit(solution)/shard_map/ppermute | solution.py:198
  40.4 0.0 collective-permute-done.11.refs_3_.refs_11_.refs_26_
  40.5 0.1 combine.25
  40.6 3.1 %collective-permute-start.15 = (bf16[32,16,256]{2,1,0:T(8,128)(2,1)S(1)}, bf16[32,16,256]{2,1,0:T(8,128)(2,1)S(1)}, u32[]{:S(2)}, u32[]{:S(2)}) collective-permute-start(bf16[32,16,256]{2,1,0:T(8,128)(2,1)S(1)} %get-tuple-element.93), channel_id=1, source_target_pairs={{0,192},{1,193},{2,194},{3,195},{4,196},{5,197},{6,198},{7,199},{8... | collective-permute-start | bytes 786440 | tf_op jit(solution)/shard_map/ppermute | solution.py:198
  43.7 0.0 collective-permute-done.12.refs_4_
  43.7 0.2 combine.26
  43.9 0.7 collective-permute-start.16
  44.6 0.6 collective-permute-done.13.refs_4_.refs_10_
  45.2 0.2 combine.27
  45.4 0.7 collective-permute-start.18
  46.1 0.1 combine.28
  46.2 1.5 %collective-permute-start.17 = (bf16[16,16,256]{2,1,0:T(8,128)(2,1)S(1)}, bf16[16,16,256]{2,1,0:T(8,128)(2,1)S(1)}, u32[]{:S(2)}, u32[]{:S(2)}) collective-permute-start(bf16[16,16,256]{2,1,0:T(8,128)(2,1)S(1)} %get-tuple-element.96), channel_id=1, source_target_pairs={{0,64},{1,65},{2,66},{3,67},{4,68},{5,69},{6,70},{7,71},{8,72},{9,... | collective-permute-start | bytes 393224 | tf_op jit(solution)/shard_map/ppermute | solution.py:198
  47.7 3.3 %collective-permute-done.15.refs_4_.refs_12_.refs_27_ = bf16[32,16,256]{2,1,0:T(8,128)(2,1)S(1)} collective-permute-done((bf16[32,16,256]{2,1,0:T(8,128)(2,1)S(1)}, bf16[32,16,256]{2,1,0:T(8,128)(2,1)S(1)}, u32[]{:S(2)}, u32[]{:S(2)}) %collective-permute-start.15) | collective-permute-done | bytes 262176 | tf_op jit(solution)/shard_map/ppermute | solution.py:198
  51.0 0.1 combine.29
  51.1 1.4 %collective-permute-start.19 = (bf16[16,16,256]{2,1,0:T(8,128)(2,1)S(1)}, bf16[16,16,256]{2,1,0:T(8,128)(2,1)S(1)}, u32[]{:S(2)}, u32[]{:S(2)}) collective-permute-start(bf16[16,16,256]{2,1,0:T(8,128)(2,1)S(1)} %get-tuple-element.99), channel_id=1, source_target_pairs={{0,1},{1,0},{2,3},{3,2},{4,5},{5,4},{6,7},{7,6},{8,9},{9,8},{10,11... | collective-permute-start | bytes 393224 | tf_op jit(solution)/shard_map/ppermute | solution.py:198
  52.5 0.0 collective-permute-done.17.refs_13_.refs_23_
  52.5 0.0 collective-permute-done.16.refs_5_
  52.5 0.2 combine.30
  52.6 3.1 %collective-permute-start.20 = (bf16[24,16,256]{2,1,0:T(8,128)(2,1)S(1)}, bf16[24,16,256]{2,1,0:T(8,128)(2,1)S(1)}, u32[]{:S(2)}, u32[]{:S(2)}) collective-permute-start(bf16[24,16,256]{2,1,0:T(8,128)(2,1)S(1)} %get-tuple-element.101), channel_id=1, source_target_pairs={{0,192},{1,193},{2,194},{3,195},{4,196},{5,197},{6,198},{7,199},{8... | collective-permute-start | bytes 589832 | tf_op jit(solution)/shard_map/ppermute | solution.py:198
  55.7 0.6 collective-permute-done.19.refs_13_.refs_28_
  56.3 0.0 collective-permute-done.18.refs_5_.refs_11_
  56.3 0.2 combine.31
  56.5 2.2 %collective-permute-start.21 = (bf16[24,16,256]{2,1,0:T(8,128)(2,1)S(1)}, bf16[24,16,256]{2,1,0:T(8,128)(2,1)S(1)}, u32[]{:S(2)}, u32[]{:S(2)}) collective-permute-start(bf16[24,16,256]{2,1,0:T(8,128)(2,1)S(1)} %get-tuple-element.102), channel_id=1, source_target_pairs={{0,3},{1,2},{2,1},{3,0},{4,7},{5,6},{6,5},{7,4},{8,11},{9,10},{10,... | collective-permute-start | bytes 589832 | tf_op jit(solution)/shard_map/ppermute | solution.py:198
  58.7 0.9 %collective-permute-done.20.refs_6_ = bf16[24,16,256]{2,1,0:T(8,128)(2,1)S(1)} collective-permute-done((bf16[24,16,256]{2,1,0:T(8,128)(2,1)S(1)}, bf16[24,16,256]{2,1,0:T(8,128)(2,1)S(1)}, u32[]{:S(2)}, u32[]{:S(2)}) %collective-permute-start.20) | collective-permute-done | bytes 196640 | tf_op jit(solution)/shard_map/ppermute | solution.py:198
  59.6 3.9 %collective-permute-done.21.refs_12_ = bf16[24,16,256]{2,1,0:T(8,128)(2,1)S(1)} collective-permute-done((bf16[24,16,256]{2,1,0:T(8,128)(2,1)S(1)}, bf16[24,16,256]{2,1,0:T(8,128)(2,1)S(1)}, u32[]{:S(2)}, u32[]{:S(2)}) %collective-permute-start.21) | collective-permute-done | bytes 196640 | tf_op jit(solution)/shard_map/ppermute | solution.py:198
  63.5 0.3 last_sends.1
  63.8 20.3 %all_to_all.5 = bf16[8,3,32,256]{3,2,1,0:T(8,128)(2,1)S(1)} all-to-all(bf16[8,3,32,256]{3,2,1,0:T(8,128)(2,1)S(1)} %last_sends.1), channel_id=1, replica_groups=mesh['y'=4,'c'=2,'z'=8,'x'=4] {'z'}, dimensions={0} | all-to-all | bytes 786432 | tf_op jit(solution)/shard_map/all_to_all | solution.py:254
  84.1 0.7 convert_reduce_fusion
  (2 shorter events, 0.0 us)
Async XLA Ops:
  6.7 7.6 %collective-permute-start = (bf16[128,16,256]{2,1,0:T(8,128)(2,1)S(1)}, bf16[128,16,256]{2,1,0:T(8,128)(2,1)S(1)}, u32[]{:S(2)}, u32[]{:S(2)}) collective-permute-start(bf16[128,16,256]{2,1,0:T(8,128)(2,1)S(1)} %get-tuple-element.60), channel_id=1, source_target_pairs={{0,32},{1,33},{2,34},{3,35},{4,36},{5,37},{6,38},{7,39},{8,40},{9,... | collective-permute-start | bytes 3145736 | tf_op jit(solution)/shard_map/ppermute | solution.py:191
  6.8 8.1 %collective-permute-start.1 = (bf16[128,16,256]{2,1,0:T(8,128)(2,1)S(1)}, bf16[128,16,256]{2,1,0:T(8,128)(2,1)S(1)}, u32[]{:S(2)}, u32[]{:S(2)}) collective-permute-start(bf16[128,16,256]{2,1,0:T(8,128)(2,1)S(1)} %get-tuple-element.63), channel_id=1, source_target_pairs={{0,32},{1,33},{2,34},{3,35},{4,36},{5,37},{6,38},{7,39},{8,40},{9,... | collective-permute-start | bytes 3145736 | tf_op jit(solution)/shard_map/ppermute | solution.py:191
  13.6 2.7 %collective-permute-start.2 = (bf16[128,16,256]{2,1,0:T(8,128)(2,1)S(1)}, bf16[128,16,256]{2,1,0:T(8,128)(2,1)S(1)}, u32[]{:S(2)}, u32[]{:S(2)}) collective-permute-start(bf16[128,16,256]{2,1,0:T(8,128)(2,1)S(1)} %get-tuple-element.66), channel_id=1, source_target_pairs={{0,32},{1,33},{2,34},{3,35},{4,36},{5,37},{6,38},{7,39},{8,40},{9,... | collective-permute-start | bytes 3145736 | tf_op jit(solution)/shard_map/ppermute | solution.py:191
  13.7 4.1 %collective-permute-start.3 = (bf16[128,16,256]{2,1,0:T(8,128)(2,1)S(1)}, bf16[128,16,256]{2,1,0:T(8,128)(2,1)S(1)}, u32[]{:S(2)}, u32[]{:S(2)}) collective-permute-start(bf16[128,16,256]{2,1,0:T(8,128)(2,1)S(1)} %get-tuple-element.69), channel_id=1, source_target_pairs={{0,32},{1,33},{2,34},{3,35},{4,36},{5,37},{6,38},{7,39},{8,40},{9,... | collective-permute-start | bytes 3145736 | tf_op jit(solution)/shard_map/ppermute | solution.py:191
  14.2 5.5 %collective-permute-start.4 = (bf16[128,16,256]{2,1,0:T(8,128)(2,1)S(1)}, bf16[128,16,256]{2,1,0:T(8,128)(2,1)S(1)}, u32[]{:S(2)}, u32[]{:S(2)}) collective-permute-start(bf16[128,16,256]{2,1,0:T(8,128)(2,1)S(1)} %get-tuple-element.72), channel_id=1, source_target_pairs={{0,32},{1,33},{2,34},{3,35},{4,36},{5,37},{6,38},{7,39},{8,40},{9,... | collective-permute-start | bytes 3145736 | tf_op jit(solution)/shard_map/ppermute | solution.py:191
  14.3 6.8 %collective-permute-start.5 = (bf16[128,16,256]{2,1,0:T(8,128)(2,1)S(1)}, bf16[128,16,256]{2,1,0:T(8,128)(2,1)S(1)}, u32[]{:S(2)}, u32[]{:S(2)}) collective-permute-start(bf16[128,16,256]{2,1,0:T(8,128)(2,1)S(1)} %get-tuple-element.75), channel_id=1, source_target_pairs={{0,32},{1,33},{2,34},{3,35},{4,36},{5,37},{6,38},{7,39},{8,40},{9,... | collective-permute-start | bytes 3145736 | tf_op jit(solution)/shard_map/ppermute | solution.py:191
  14.9 9.4 %collective-permute-start.6 = (bf16[64,16,256]{2,1,0:T(8,128)(2,1)S(1)}, bf16[64,16,256]{2,1,0:T(8,128)(2,1)S(1)}, u32[]{:S(2)}, u32[]{:S(2)}) collective-permute-start(bf16[64,16,256]{2,1,0:T(8,128)(2,1)S(1)} %get-tuple-element.77), channel_id=1, source_target_pairs={{0,1},{1,0},{2,3},{3,2},{4,5},{5,4},{6,7},{7,6},{8,9},{9,8},{10,11... | collective-permute-start | bytes 1572872 | tf_op jit(solution)/shard_map/ppermute | solution.py:198
  16.5 13.4 %collective-permute-start.7 = (bf16[64,16,256]{2,1,0:T(8,128)(2,1)S(1)}, bf16[64,16,256]{2,1,0:T(8,128)(2,1)S(1)}, u32[]{:S(2)}, u32[]{:S(2)}) collective-permute-start(bf16[64,16,256]{2,1,0:T(8,128)(2,1)S(1)} %get-tuple-element.78), channel_id=1, source_target_pairs={{0,1},{1,0},{2,3},{3,2},{4,5},{5,4},{6,7},{7,6},{8,9},{9,8},{10,11... | collective-permute-start | bytes 1572872 | tf_op jit(solution)/shard_map/ppermute | solution.py:198
  18.0 14.5 %collective-permute-start.9 = (bf16[64,16,256]{2,1,0:T(8,128)(2,1)S(1)}, bf16[64,16,256]{2,1,0:T(8,128)(2,1)S(1)}, u32[]{:S(2)}, u32[]{:S(2)}) collective-permute-start(bf16[64,16,256]{2,1,0:T(8,128)(2,1)S(1)} %get-tuple-element.81), channel_id=1, source_target_pairs={{0,64},{1,65},{2,66},{3,67},{4,68},{5,69},{6,70},{7,71},{8,72},{9,... | collective-permute-start | bytes 1572872 | tf_op jit(solution)/shard_map/ppermute | solution.py:198
  19.7 13.2 %collective-permute-start.8 = (bf16[64,16,256]{2,1,0:T(8,128)(2,1)S(1)}, bf16[64,16,256]{2,1,0:T(8,128)(2,1)S(1)}, u32[]{:S(2)}, u32[]{:S(2)}) collective-permute-start(bf16[64,16,256]{2,1,0:T(8,128)(2,1)S(1)} %get-tuple-element.80), channel_id=1, source_target_pairs={{0,64},{1,65},{2,66},{3,67},{4,68},{5,69},{6,70},{7,71},{8,72},{9,... | collective-permute-start | bytes 1572872 | tf_op jit(solution)/shard_map/ppermute | solution.py:198
  21.1 16.9 %collective-permute-start.10 = (bf16[64,16,256]{2,1,0:T(8,128)(2,1)S(1)}, bf16[64,16,256]{2,1,0:T(8,128)(2,1)S(1)}, u32[]{:S(2)}, u32[]{:S(2)}) collective-permute-start(bf16[64,16,256]{2,1,0:T(8,128)(2,1)S(1)} %get-tuple-element.83), channel_id=1, source_target_pairs={{0,1},{1,0},{2,3},{3,2},{4,5},{5,4},{6,7},{7,6},{8,9},{9,8},{10,11... | collective-permute-start | bytes 1572872 | tf_op jit(solution)/shard_map/ppermute | solution.py:198
  24.3 16.1 %collective-permute-start.11 = (bf16[64,16,256]{2,1,0:T(8,128)(2,1)S(1)}, bf16[64,16,256]{2,1,0:T(8,128)(2,1)S(1)}, u32[]{:S(2)}, u32[]{:S(2)}) collective-permute-start(bf16[64,16,256]{2,1,0:T(8,128)(2,1)S(1)} %get-tuple-element.85), channel_id=1, source_target_pairs={{0,64},{1,65},{2,66},{3,67},{4,68},{5,69},{6,70},{7,71},{8,72},{9,... | collective-permute-start | bytes 1572872 | tf_op jit(solution)/shard_map/ppermute | solution.py:198
  30.2 13.5 %collective-permute-start.12 = (bf16[64,16,256]{2,1,0:T(8,128)(2,1)S(1)}, bf16[64,16,256]{2,1,0:T(8,128)(2,1)S(1)}, u32[]{:S(2)}, u32[]{:S(2)}) collective-permute-start(bf16[64,16,256]{2,1,0:T(8,128)(2,1)S(1)} %get-tuple-element.87), channel_id=1, source_target_pairs={{0,3},{1,2},{2,1},{3,0},{4,7},{5,6},{6,5},{7,4},{8,11},{9,10},{10,... | collective-permute-start | bytes 1572872 | tf_op jit(solution)/shard_map/ppermute | solution.py:198
  33.2 12.1 %collective-permute-start.13 = (bf16[64,16,256]{2,1,0:T(8,128)(2,1)S(1)}, bf16[64,16,256]{2,1,0:T(8,128)(2,1)S(1)}, u32[]{:S(2)}, u32[]{:S(2)}) collective-permute-start(bf16[64,16,256]{2,1,0:T(8,128)(2,1)S(1)} %get-tuple-element.89), channel_id=1, source_target_pairs={{0,192},{1,193},{2,194},{3,195},{4,196},{5,197},{6,198},{7,199},{8... | collective-permute-start | bytes 1572872 | tf_op jit(solution)/shard_map/ppermute | solution.py:198
  38.1 8.0 %collective-permute-start.14 = (bf16[32,16,256]{2,1,0:T(8,128)(2,1)S(1)}, bf16[32,16,256]{2,1,0:T(8,128)(2,1)S(1)}, u32[]{:S(2)}, u32[]{:S(2)}) collective-permute-start(bf16[32,16,256]{2,1,0:T(8,128)(2,1)S(1)} %get-tuple-element.91), channel_id=1, source_target_pairs={{0,3},{1,2},{2,1},{3,0},{4,7},{5,6},{6,5},{7,4},{8,11},{9,10},{10,... | collective-permute-start | bytes 786440 | tf_op jit(solution)/shard_map/ppermute | solution.py:198
  40.6 10.4 %collective-permute-start.15 = (bf16[32,16,256]{2,1,0:T(8,128)(2,1)S(1)}, bf16[32,16,256]{2,1,0:T(8,128)(2,1)S(1)}, u32[]{:S(2)}, u32[]{:S(2)}) collective-permute-start(bf16[32,16,256]{2,1,0:T(8,128)(2,1)S(1)} %get-tuple-element.93), channel_id=1, source_target_pairs={{0,192},{1,193},{2,194},{3,195},{4,196},{5,197},{6,198},{7,199},{8... | collective-permute-start | bytes 786440 | tf_op jit(solution)/shard_map/ppermute | solution.py:198
  43.9 8.6 %collective-permute-start.16 = (bf16[32,16,256]{2,1,0:T(8,128)(2,1)S(1)}, bf16[32,16,256]{2,1,0:T(8,128)(2,1)S(1)}, u32[]{:S(2)}, u32[]{:S(2)}) collective-permute-start(bf16[32,16,256]{2,1,0:T(8,128)(2,1)S(1)} %get-tuple-element.95), channel_id=1, source_target_pairs={{0,64},{1,65},{2,66},{3,67},{4,68},{5,69},{6,70},{7,71},{8,72},{9,... | collective-permute-start | bytes 786440 | tf_op jit(solution)/shard_map/ppermute | solution.py:198
  45.4 10.9 %collective-permute-start.18 = (bf16[32,16,256]{2,1,0:T(8,128)(2,1)S(1)}, bf16[32,16,256]{2,1,0:T(8,128)(2,1)S(1)}, u32[]{:S(2)}, u32[]{:S(2)}) collective-permute-start(bf16[32,16,256]{2,1,0:T(8,128)(2,1)S(1)} %get-tuple-element.98), channel_id=1, source_target_pairs={{0,1},{1,0},{2,3},{3,2},{4,5},{5,4},{6,7},{7,6},{8,9},{9,8},{10,11... | collective-permute-start | bytes 786440 | tf_op jit(solution)/shard_map/ppermute | solution.py:198
  46.2 6.3 %collective-permute-start.17 = (bf16[16,16,256]{2,1,0:T(8,128)(2,1)S(1)}, bf16[16,16,256]{2,1,0:T(8,128)(2,1)S(1)}, u32[]{:S(2)}, u32[]{:S(2)}) collective-permute-start(bf16[16,16,256]{2,1,0:T(8,128)(2,1)S(1)} %get-tuple-element.96), channel_id=1, source_target_pairs={{0,64},{1,65},{2,66},{3,67},{4,68},{5,69},{6,70},{7,71},{8,72},{9,... | collective-permute-start | bytes 393224 | tf_op jit(solution)/shard_map/ppermute | solution.py:198
  51.1 5.2 %collective-permute-start.19 = (bf16[16,16,256]{2,1,0:T(8,128)(2,1)S(1)}, bf16[16,16,256]{2,1,0:T(8,128)(2,1)S(1)}, u32[]{:S(2)}, u32[]{:S(2)}) collective-permute-start(bf16[16,16,256]{2,1,0:T(8,128)(2,1)S(1)} %get-tuple-element.99), channel_id=1, source_target_pairs={{0,1},{1,0},{2,3},{3,2},{4,5},{5,4},{6,7},{7,6},{8,9},{9,8},{10,11... | collective-permute-start | bytes 393224 | tf_op jit(solution)/shard_map/ppermute | solution.py:198
  52.6 7.0 %collective-permute-start.20 = (bf16[24,16,256]{2,1,0:T(8,128)(2,1)S(1)}, bf16[24,16,256]{2,1,0:T(8,128)(2,1)S(1)}, u32[]{:S(2)}, u32[]{:S(2)}) collective-permute-start(bf16[24,16,256]{2,1,0:T(8,128)(2,1)S(1)} %get-tuple-element.101), channel_id=1, source_target_pairs={{0,192},{1,193},{2,194},{3,195},{4,196},{5,197},{6,198},{7,199},{8... | collective-permute-start | bytes 589832 | tf_op jit(solution)/shard_map/ppermute | solution.py:198
  56.5 7.0 %collective-permute-start.21 = (bf16[24,16,256]{2,1,0:T(8,128)(2,1)S(1)}, bf16[24,16,256]{2,1,0:T(8,128)(2,1)S(1)}, u32[]{:S(2)}, u32[]{:S(2)}) collective-permute-start(bf16[24,16,256]{2,1,0:T(8,128)(2,1)S(1)} %get-tuple-element.102), channel_id=1, source_target_pairs={{0,3},{1,2},{2,1},{3,0},{4,7},{5,6},{6,5},{7,4},{8,11},{9,10},{10,... | collective-permute-start | bytes 589832 | tf_op jit(solution)/shard_map/ppermute | solution.py:198

commit v3 on v2

--- a/solution.py
+++ b/solution.py
@@ -61,7 +61,7 @@
             (((1,), (1,)), ((), ())),
             preferred_element_type=jnp.float32,
         )
-        target = target_ref[0, first + t, 0]
+        target = target_ref[first + t]
         for i in range(2 * len(vectors)):
             part = 2 * vectors[0] + i
             for other, ref in enumerate((keeps[i], sends[i])):
@@ -112,6 +112,7 @@
 
 TOKEN = jax.ShapeDtypeStruct((8, 128), jnp.float32)
 LIMIT = pltpu.CompilerParams(vmem_limit_bytes=24 * 2**20)
+LONG = pl.CostEstimate(flops=10**11, bytes_accessed=1, transcendentals=0)
 SMALL = pl.CostEstimate(flops=1, bytes_accessed=1, transcendentals=0)
 
 
@@ -175,6 +176,22 @@
     )(token, *arrays)
 
 
+def absorb_kernel(after_ref, got_ref, token_ref):
+    token_ref[...] = jnp.zeros_like(token_ref)
+
+
+def absorb(token, got, cost):
+    return pl.pallas_call(
+        absorb_kernel,
+        in_specs=[ANY, ANY],
+        out_specs=VMEM,
+        out_shape=TOKEN,
+        compiler_params=LIMIT,
+        cost_estimate=cost,
+        name="absorb",
+    )(token, got)
+
+
 def permutation(move):
     pairs = []
     for index in range(256):
@@ -221,11 +238,13 @@
     )(token, *arrays)
 
 
-ORDER = [
-    (1, (0,)), (1, (1,)), (1, (2,)), (1, (3,)), (1, (4,)), (1, (5,)),
+WAIT, LONG_WAIT = 0, -1
+EARLY = [(1, (0,)), (1, (1,))]
+LATE = [
+    (1, (2,)), (1, (3,)), (WAIT, (0,)), (LONG_WAIT, (1,)), (1, (4,)), (1, (5,)),
     (2, (0, 2)), (2, (1, 3)), (2, (4,)), (2, (5,)),
-    (3, (0, 2)), (3, (1, 3)), (3, (4,)), (3, (5,)),
-    (4, (0, 2, 4)), (4, (1, 3, 5)),
+    (3, (0, 2)), (3, (1, 3)), (3, (4,)), (3, (5,)), (WAIT, (0,)), (WAIT, (1,)),
+    (4, (0, 2, 4)), (4, (1, 3, 5)), (WAIT, (0,)),
 ]
 
 
@@ -238,6 +257,9 @@
 
     def run(token, order):
         for step, members in order:
+            if step in (WAIT, LONG_WAIT):
+                token = absorb(token, parts[members[0]][-1][0], LONG if step == LONG_WAIT else SMALL)
+                continue
             n = 128 >> step
             out, token = combine(token, n, [[(a, at + n) for a, at in parts[p]] for p in members])
             along_x = (members[0] % 2 == 0) == (step <= 2)
@@ -246,11 +268,15 @@
                 parts[p].append((got, i * n))
         return token
 
-    *sums, token, psi, left, right = first_products(target_sector, wavefunction, left_operators, right_operators)
+    target = target_sector.reshape(TERMS)
+    *sums, token, psi, left, right = first_products(target, wavefunction, left_operators, right_operators)
     start(sums)
-    *sums, token = later_products(token, (1, 2), target_sector, psi, left, right)
+    *sums, token = later_products(token, (1,), target, psi, left, right)
     start(sums)
-    token = run(token, ORDER)
+    token = run(token, EARLY)
+    *sums, token = later_products(token, (2,), target, psi, left, right)
+    start(sums)
+    token = run(token, LATE)
     spread = lax.all_to_all(last_sends(token, parts), "z", 0, 0, tiled=True)
     return jnp.sum(spread.astype(jnp.float32), axis=0)[None]
 

time: 85 us -> 83.5 us (0.982)
  starting transfers between devices: 29.7 us -> 27.7 us
    ppermute x16, starting transfers between devices: 28 us -> 25.7 us  [swap(): return lax.ppermute(a, AXES, permutation(move))]
    ppermute x16, waiting for transfers between devices: 17.7 us -> 18.7 us  [swap(): return lax.ppermute(a, AXES, permutation(move))]
    pallas_call x1 -> x2, Pallas kernels: 6.28 us -> 6.46 us  [later_products(): pl.pallas_call(functools.partial(later_kernel, vectors), in_specs=[ANY, S...]
  transfers between devices with their start and end apart: 22 -> 22, of which waited for: 11 -> 8; matrix products, arithmetic and copies ran while one was open for 0% -> 0% of each run, Pallas kernels for 11% -> 11%
where the time goes in v3:
time: 83.5 us; the launch traced here: 83.4 us
  starting transfers between devices  27.7 us (33%)
  blocking collectives  20.1 us (24%)
  waiting for transfers between devices  18.8 us (23%)
  Pallas kernels  15.2 us (18%)
    ppermute x16, starting transfers between devices, swap(): return lax.ppermute(a, AXES, permutation(move))  25.7 us
    all_to_all x1, blocking collectives, body(): spread = lax.all_to_all(last_sends(token, parts), 'z', 0, 0, tiled=True)  20.1 us
    ppermute x16, waiting for transfers between devices, swap(): return lax.ppermute(a, AXES, permutation(move))  18.7 us
    pallas_call x2, Pallas kernels, later_products(): pl.pallas_call(functools.partial(later_kernel, vectors), in_specs=[ANY, S...  6.46 us
    pallas_call x1, Pallas kernels, first_products(): pl.pallas_call(first_kernel, in_specs=[SMEM, HBM, HBM, HBM], out_specs=[V...  5.69 us
    pallas_call x16, Pallas kernels, combine(): pl.pallas_call(functools.partial(combine_kernel, n, places), in_specs=[AN...  2.7 us
    ppermute x6, starting transfers between devices, core_swap(): lax.ppermute(a, AXES, permutation(lambda y, c, z, x: (y, 1 - c, z, x)))  2.01 us
  transfers between devices with their start and end apart: 22, of which 8 were waited for; matrix products, arithmetic and copies ran while one was open for 0% of the time, Pallas kernels for 11%

profile of v3, /device:TPU:6, one launch (start us, length us, event | category | flops | bytes accessed | tf_op | source)
XLA Modules:
  0.0 83.4 jit_solution(12985668855493527948)
XLA Ops:
  0.0 0.7 copy-done
  0.7 5.7 %first_products.1 = (bf16[128,16,256]{2,1,0:T(8,128)(2,1)S(1)}, bf16[128,16,256]{2,1,0:T(8,128)(2,1)S(1)}, bf16[128,16,256]{2,1,0:T(8,128)(2,1)S(1)}, bf16[128,1...) custom-call(s32[32]{0:T(128)S(1)} %bitcast.2, ...), custom_call_target="tpu_custom_call" | custom-call | flops 1 | bytes 1 | tf_op jit(solution)/shard_map/first_products/pallas_call | solution.py:121
  6.4 0.1 collective-permute-start
  6.5 0.5 collective-permute-start.1
  7.0 3.2 %later_products.2 = (bf16[128,16,256]{2,1,0:T(8,128)(2,1)S(1)}, bf16[128,16,256]{2,1,0:T(8,128)(2,1)S(1)}, bf16[128,16,256]{2,1,0:T(8,128)(2,1)S(1)}, bf16[128,16,256]{2,1,0:T(8,128)(2,1)S(1)}, f32[8,128]{1,0:T(8,128)S(1)}) custom-call(f32[8,128]{1,0:T(8,128)S(1)} %get-tuple-element.55.after_ref, s32[32]{0:T(128)S(1)} %bitcast.3, ...), custom_call_target="tpu_custom_call" | custom-call | flops 1 | bytes 1 | tf_op jit(solution)/shard_map/later_products/pallas_call | solution.py:134
  10.2 0.2 collective-permute-start.2
  10.4 0.4 collective-permute-start.3
  10.8 0.2 combine.16
  11.0 0.9 %collective-permute-start.4 = (bf16[64,16,256]{2,1,0:T(8,128)(2,1)S(1)}, bf16[64,16,256]{2,1,0:T(8,128)(2,1)S(1)}, u32[]{:S(2)}, u32[]{:S(2)}) collective-permute-start(bf16[64,16,256]{2,1,0:T(8,128)(2,1)S(1)} %get-tuple-element.73), channel_id=1, source_target_pairs={{0,1},{1,0},{2,3},{3,2},{4,5},{5,4},{6,7},{7,6},{8,9},{9,8},{10,11... | collective-permute-start | bytes 1572872 | tf_op jit(solution)/shard_map/ppermute | solution.py:215
  11.9 0.2 combine.17
  12.1 1.8 %collective-permute-start.5 = (bf16[64,16,256]{2,1,0:T(8,128)(2,1)S(1)}, bf16[64,16,256]{2,1,0:T(8,128)(2,1)S(1)}, u32[]{:S(2)}, u32[]{:S(2)}) collective-permute-start(bf16[64,16,256]{2,1,0:T(8,128)(2,1)S(1)} %get-tuple-element.74), channel_id=1, source_target_pairs={{0,64},{1,65},{2,66},{3,67},{4,68},{5,69},{6,70},{7,71},{8,72},{9,... | collective-permute-start | bytes 1572872 | tf_op jit(solution)/shard_map/ppermute | solution.py:215
  13.9 3.2 %later_products.3 = (bf16[128,16,256]{2,1,0:T(8,128)(2,1)S(1)}, bf16[128,16,256]{2,1,0:T(8,128)(2,1)S(1)}, bf16[128,16,256]{2,1,0:T(8,128)(2,1)S(1)}, bf16[128,16,256]{2,1,0:T(8,128)(2,1)S(1)}, f32[8,128]{1,0:T(8,128)S(1)}) custom-call(f32[8,128]{1,0:T(8,128)S(1)} %get-tuple-element.65.after_ref, s32[32]{0:T(128)S(1)} %bitcast.4, ...), custom_call_target="tpu_custom_call" | custom-call | flops 1 | bytes 1 | tf_op jit(solution)/shard_map/later_products/pallas_call | solution.py:134
  17.2 0.7 collective-permute-start.6
  17.9 0.1 collective-permute-start.7
  18.0 0.2 combine.18
  18.2 0.0 collective-permute-done.3.refs_2_.refs_5_.refs_6_.refs_7_.refs_17_
  18.2 1.1 %collective-permute-start.8 = (bf16[64,16,256]{2,1,0:T(8,128)(2,1)S(1)}, bf16[64,16,256]{2,1,0:T(8,128)(2,1)S(1)}, u32[]{:S(2)}, u32[]{:S(2)}) collective-permute-start(bf16[64,16,256]{2,1,0:T(8,128)(2,1)S(1)} %get-tuple-element.81), channel_id=1, source_target_pairs={{0,1},{1,0},{2,3},{3,2},{4,5},{5,4},{6,7},{7,6},{8,9},{9,8},{10,11... | collective-permute-start | bytes 1572872 | tf_op jit(solution)/shard_map/ppermute | solution.py:215
  19.3 0.2 combine.19
  19.4 0.8 collective-permute-done.4.got_ref.refs_3_
  20.3 1.6 %collective-permute-start.9 = (bf16[64,16,256]{2,1,0:T(8,128)(2,1)S(1)}, bf16[64,16,256]{2,1,0:T(8,128)(2,1)S(1)}, u32[]{:S(2)}, u32[]{:S(2)}) collective-permute-start(bf16[64,16,256]{2,1,0:T(8,128)(2,1)S(1)} %get-tuple-element.83), channel_id=1, source_target_pairs={{0,64},{1,65},{2,66},{3,67},{4,68},{5,69},{6,70},{7,71},{8,72},{9,... | collective-permute-start | bytes 1572872 | tf_op jit(solution)/shard_map/ppermute | solution.py:215
  21.8 0.0 collective-permute-done.5.got_ref.refs_3_.refs_9_
  21.8 0.0 collective-permute-done.6.refs_2_.refs_10_.refs_20_
  21.8 0.2 combine.20
  22.0 1.0 %collective-permute-start.10 = (bf16[64,16,256]{2,1,0:T(8,128)(2,1)S(1)}, bf16[64,16,256]{2,1,0:T(8,128)(2,1)S(1)}, u32[]{:S(2)}, u32[]{:S(2)}) collective-permute-start(bf16[64,16,256]{2,1,0:T(8,128)(2,1)S(1)} %get-tuple-element.85), channel_id=1, source_target_pairs={{0,1},{1,0},{2,3},{3,2},{4,5},{5,4},{6,7},{7,6},{8,9},{9,8},{10,11... | collective-permute-start | bytes 1572872 | tf_op jit(solution)/shard_map/ppermute | solution.py:215
  23.0 0.0 collective-permute-done.7.refs_2_.refs_10_.refs_25_
  23.0 0.2 combine.21
  23.2 1.7 %collective-permute-start.11 = (bf16[64,16,256]{2,1,0:T(8,128)(2,1)S(1)}, bf16[64,16,256]{2,1,0:T(8,128)(2,1)S(1)}, u32[]{:S(2)}, u32[]{:S(2)}) collective-permute-start(bf16[64,16,256]{2,1,0:T(8,128)(2,1)S(1)} %get-tuple-element.87), channel_id=1, source_target_pairs={{0,64},{1,65},{2,66},{3,67},{4,68},{5,69},{6,70},{7,71},{8,72},{9,... | collective-permute-start | bytes 1572872 | tf_op jit(solution)/shard_map/ppermute | solution.py:215
  24.9 2.6 %collective-permute-done.8.refs_6_.refs_7_.refs_8_.refs_15_ = bf16[64,16,256]{2,1,0:T(8,128)(2,1)S(1)} collective-permute-done((bf16[64,16,256]{2,1,0:T(8,128)(2,1)S(1)}, bf16[64,16,256]{2,1,0:T(8,128)(2,1)S(1)}, u32[]{:S(2)}, u32[]{:S(2)}) %collective-permute-start.8) | collective-permute-done | bytes 524320 | tf_op jit(solution)/shard_map/ppermute | solution.py:215
  27.5 0.3 combine.22
  27.7 2.9 %collective-permute-start.12 = (bf16[64,16,256]{2,1,0:T(8,128)(2,1)S(1)}, bf16[64,16,256]{2,1,0:T(8,128)(2,1)S(1)}, u32[]{:S(2)}, u32[]{:S(2)}) collective-permute-start(bf16[64,16,256]{2,1,0:T(8,128)(2,1)S(1)} %get-tuple-element.89), channel_id=1, source_target_pairs={{0,3},{1,2},{2,1},{3,0},{4,7},{5,6},{6,5},{7,4},{8,11},{9,10},{10,... | collective-permute-start | bytes 1572872 | tf_op jit(solution)/shard_map/ppermute | solution.py:215
  30.6 0.0 collective-permute-done.9.refs_6_.refs_7_.refs_8_.refs_18_
  30.6 0.3 combine.23
  30.9 1.9 %collective-permute-start.13 = (bf16[64,16,256]{2,1,0:T(8,128)(2,1)S(1)}, bf16[64,16,256]{2,1,0:T(8,128)(2,1)S(1)}, u32[]{:S(2)}, u32[]{:S(2)}) collective-permute-start(bf16[64,16,256]{2,1,0:T(8,128)(2,1)S(1)} %get-tuple-element.91), channel_id=1, source_target_pairs={{0,192},{1,193},{2,194},{3,195},{4,196},{5,197},{6,198},{7,199},{8... | collective-permute-start | bytes 1572872 | tf_op jit(solution)/shard_map/ppermute | solution.py:215
  32.8 2.4 %collective-permute-done.10.refs_3_.refs_11_.refs_21_ = bf16[64,16,256]{2,1,0:T(8,128)(2,1)S(1)} collective-permute-done((bf16[64,16,256]{2,1,0:T(8,128)(2,1)S(1)}, bf16[64,16,256]{2,1,0:T(8,128)(2,1)S(1)}, u32[]{:S(2)}, u32[]{:S(2)}) %collective-permute-start.10) | collective-permute-done | bytes 524320 | tf_op jit(solution)/shard_map/ppermute | solution.py:215
  35.2 0.1 combine.24
  35.4 2.9 %collective-permute-start.14 = (bf16[32,16,256]{2,1,0:T(8,128)(2,1)S(1)}, bf16[32,16,256]{2,1,0:T(8,128)(2,1)S(1)}, u32[]{:S(2)}, u32[]{:S(2)}) collective-permute-start(bf16[32,16,256]{2,1,0:T(8,128)(2,1)S(1)} %get-tuple-element.93), channel_id=1, source_target_pairs={{0,3},{1,2},{2,1},{3,0},{4,7},{5,6},{6,5},{7,4},{8,11},{9,10},{10,... | collective-permute-start | bytes 786440 | tf_op jit(solution)/shard_map/ppermute | solution.py:215
  38.2 0.0 collective-permute-done.11.refs_3_.refs_11_.refs_26_
  38.2 0.1 combine.25
  38.3 2.3 %collective-permute-start.15 = (bf16[32,16,256]{2,1,0:T(8,128)(2,1)S(1)}, bf16[32,16,256]{2,1,0:T(8,128)(2,1)S(1)}, u32[]{:S(2)}, u32[]{:S(2)}) collective-permute-start(bf16[32,16,256]{2,1,0:T(8,128)(2,1)S(1)} %get-tuple-element.95), channel_id=1, source_target_pairs={{0,192},{1,193},{2,194},{3,195},{4,196},{5,197},{6,198},{7,199},{8... | collective-permute-start | bytes 786440 | tf_op jit(solution)/shard_map/ppermute | solution.py:215
  40.7 0.0 collective-permute-done.12.refs_4_
  40.7 0.2 combine.26
  40.9 0.7 collective-permute-start.16
  41.5 0.6 collective-permute-done.13.refs_4_.refs_10_
  42.1 0.2 combine.27
  42.3 1.1 %collective-permute-start.17 = (bf16[32,16,256]{2,1,0:T(8,128)(2,1)S(1)}, bf16[32,16,256]{2,1,0:T(8,128)(2,1)S(1)}, u32[]{:S(2)}, u32[]{:S(2)}) collective-permute-start(bf16[32,16,256]{2,1,0:T(8,128)(2,1)S(1)} %get-tuple-element.98), channel_id=1, source_target_pairs={{0,1},{1,0},{2,3},{3,2},{4,5},{5,4},{6,7},{7,6},{8,9},{9,8},{10,11... | collective-permute-start | bytes 786440 | tf_op jit(solution)/shard_map/ppermute | solution.py:215
  43.4 0.0 collective-permute-done.14.refs_4_.refs_12_.refs_22_
  43.4 0.1 combine.28
  43.5 1.6 %collective-permute-start.18 = (bf16[16,16,256]{2,1,0:T(8,128)(2,1)S(1)}, bf16[16,16,256]{2,1,0:T(8,128)(2,1)S(1)}, u32[]{:S(2)}, u32[]{:S(2)}) collective-permute-start(bf16[16,16,256]{2,1,0:T(8,128)(2,1)S(1)} %get-tuple-element.99), channel_id=1, source_target_pairs={{0,64},{1,65},{2,66},{3,67},{4,68},{5,69},{6,70},{7,71},{8,72},{9,... | collective-permute-start | bytes 393224 | tf_op jit(solution)/shard_map/ppermute | solution.py:215
  45.2 3.7 %collective-permute-done.15.refs_4_.refs_12_.refs_27_ = bf16[32,16,256]{2,1,0:T(8,128)(2,1)S(1)} collective-permute-done((bf16[32,16,256]{2,1,0:T(8,128)(2,1)S(1)}, bf16[32,16,256]{2,1,0:T(8,128)(2,1)S(1)}, u32[]{:S(2)}, u32[]{:S(2)}) %collective-permute-start.15) | collective-permute-done | bytes 262176 | tf_op jit(solution)/shard_map/ppermute | solution.py:215
  48.8 0.1 combine.29
  48.9 0.8 %collective-permute-start.19 = (bf16[16,16,256]{2,1,0:T(8,128)(2,1)S(1)}, bf16[16,16,256]{2,1,0:T(8,128)(2,1)S(1)}, u32[]{:S(2)}, u32[]{:S(2)}) collective-permute-start(bf16[16,16,256]{2,1,0:T(8,128)(2,1)S(1)} %get-tuple-element.101), channel_id=1, source_target_pairs={{0,1},{1,0},{2,3},{3,2},{4,5},{5,4},{6,7},{7,6},{8,9},{9,8},{10,11... | collective-permute-start | bytes 393224 | tf_op jit(solution)/shard_map/ppermute | solution.py:215
  49.7 0.0 collective-permute-done.16.got_ref.refs_5_
  49.8 0.0 collective-permute-done.17.got_ref.refs_5_.refs_11_
  49.8 0.0 collective-permute-done.18.refs_13_.refs_23_
  49.8 0.2 combine.30
  49.9 3.3 %collective-permute-start.20 = (bf16[24,16,256]{2,1,0:T(8,128)(2,1)S(1)}, bf16[24,16,256]{2,1,0:T(8,128)(2,1)S(1)}, u32[]{:S(2)}, u32[]{:S(2)}) collective-permute-start(bf16[24,16,256]{2,1,0:T(8,128)(2,1)S(1)} %get-tuple-element.103), channel_id=1, source_target_pairs={{0,192},{1,193},{2,194},{3,195},{4,196},{5,197},{6,198},{7,199},{8... | collective-permute-start | bytes 589832 | tf_op jit(solution)/shard_map/ppermute | solution.py:215
  53.3 1.8 %collective-permute-done.19.refs_13_.refs_28_ = bf16[16,16,256]{2,1,0:T(8,128)(2,1)S(1)} collective-permute-done((bf16[16,16,256]{2,1,0:T(8,128)(2,1)S(1)}, bf16[16,16,256]{2,1,0:T(8,128)(2,1)S(1)}, u32[]{:S(2)}, u32[]{:S(2)}) %collective-permute-start.19) | collective-permute-done | bytes 131104 | tf_op jit(solution)/shard_map/ppermute | solution.py:215
  55.1 0.1 combine.31
  55.2 0.1 collective-permute-start.21
  55.3 1.6 %collective-permute-done.20.got_ref.refs_6_ = bf16[24,16,256]{2,1,0:T(8,128)(2,1)S(1)} collective-permute-done((bf16[24,16,256]{2,1,0:T(8,128)(2,1)S(1)}, bf16[24,16,256]{2,1,0:T(8,128)(2,1)S(1)}, u32[]{:S(2)}, u32[]{:S(2)}) %collective-permute-start.20) | collective-permute-done | bytes 196640 | tf_op jit(solution)/shard_map/ppermute | solution.py:215
  56.9 5.3 %collective-permute-done.21.refs_12_ = bf16[24,16,256]{2,1,0:T(8,128)(2,1)S(1)} collective-permute-done((bf16[24,16,256]{2,1,0:T(8,128)(2,1)S(1)}, bf16[24,16,256]{2,1,0:T(8,128)(2,1)S(1)}, u32[]{:S(2)}, u32[]{:S(2)}) %collective-permute-start.21) | collective-permute-done | bytes 196640 | tf_op jit(solution)/shard_map/ppermute | solution.py:215
  62.2 0.3 last_sends.1
  62.6 20.1 %all_to_all.5 = bf16[8,3,32,256]{3,2,1,0:T(8,128)(2,1)S(1)} all-to-all(bf16[8,3,32,256]{3,2,1,0:T(8,128)(2,1)S(1)} %last_sends.1), channel_id=1, replica_groups=mesh['y'=4,'c'=2,'z'=8,'x'=4] {'z'}, dimensions={0} | all-to-all | bytes 786432 | tf_op jit(solution)/shard_map/all_to_all | solution.py:280
  82.7 0.7 convert_reduce_fusion
  (9 shorter events, 0.0 us)
Async XLA Ops:
  0.0 0.7 copy-start
  6.4 4.4 %collective-permute-start = (bf16[128,16,256]{2,1,0:T(8,128)(2,1)S(1)}, bf16[128,16,256]{2,1,0:T(8,128)(2,1)S(1)}, u32[]{:S(2)}, u32[]{:S(2)}) collective-permute-start(bf16[128,16,256]{2,1,0:T(8,128)(2,1)S(1)} %get-tuple-element.61), channel_id=1, source_target_pairs={{0,32},{1,33},{2,34},{3,35},{4,36},{5,37},{6,38},{7,39},{8,40},{9,... | collective-permute-start | bytes 3145736 | tf_op jit(solution)/shard_map/ppermute | solution.py:208
  6.5 5.4 %collective-permute-start.1 = (bf16[128,16,256]{2,1,0:T(8,128)(2,1)S(1)}, bf16[128,16,256]{2,1,0:T(8,128)(2,1)S(1)}, u32[]{:S(2)}, u32[]{:S(2)}) collective-permute-start(bf16[128,16,256]{2,1,0:T(8,128)(2,1)S(1)} %get-tuple-element.64), channel_id=1, source_target_pairs={{0,32},{1,33},{2,34},{3,35},{4,36},{5,37},{6,38},{7,39},{8,40},{9,... | collective-permute-start | bytes 3145736 | tf_op jit(solution)/shard_map/ppermute | solution.py:208
  10.2 7.7 %collective-permute-start.2 = (bf16[128,16,256]{2,1,0:T(8,128)(2,1)S(1)}, bf16[128,16,256]{2,1,0:T(8,128)(2,1)S(1)}, u32[]{:S(2)}, u32[]{:S(2)}) collective-permute-start(bf16[128,16,256]{2,1,0:T(8,128)(2,1)S(1)} %get-tuple-element.68), channel_id=1, source_target_pairs={{0,32},{1,33},{2,34},{3,35},{4,36},{5,37},{6,38},{7,39},{8,40},{9,... | collective-permute-start | bytes 3145736 | tf_op jit(solution)/shard_map/ppermute | solution.py:208
  10.4 7.8 %collective-permute-start.3 = (bf16[128,16,256]{2,1,0:T(8,128)(2,1)S(1)}, bf16[128,16,256]{2,1,0:T(8,128)(2,1)S(1)}, u32[]{:S(2)}, u32[]{:S(2)}) collective-permute-start(bf16[128,16,256]{2,1,0:T(8,128)(2,1)S(1)} %get-tuple-element.71), channel_id=1, source_target_pairs={{0,32},{1,33},{2,34},{3,35},{4,36},{5,37},{6,38},{7,39},{8,40},{9,... | collective-permute-start | bytes 3145736 | tf_op jit(solution)/shard_map/ppermute | solution.py:208
  11.0 9.3 %collective-permute-start.4 = (bf16[64,16,256]{2,1,0:T(8,128)(2,1)S(1)}, bf16[64,16,256]{2,1,0:T(8,128)(2,1)S(1)}, u32[]{:S(2)}, u32[]{:S(2)}) collective-permute-start(bf16[64,16,256]{2,1,0:T(8,128)(2,1)S(1)} %get-tuple-element.73), channel_id=1, source_target_pairs={{0,1},{1,0},{2,3},{3,2},{4,5},{5,4},{6,7},{7,6},{8,9},{9,8},{10,11... | collective-permute-start | bytes 1572872 | tf_op jit(solution)/shard_map/ppermute | solution.py:215
  12.1 9.7 %collective-permute-start.5 = (bf16[64,16,256]{2,1,0:T(8,128)(2,1)S(1)}, bf16[64,16,256]{2,1,0:T(8,128)(2,1)S(1)}, u32[]{:S(2)}, u32[]{:S(2)}) collective-permute-start(bf16[64,16,256]{2,1,0:T(8,128)(2,1)S(1)} %get-tuple-element.74), channel_id=1, source_target_pairs={{0,64},{1,65},{2,66},{3,67},{4,68},{5,69},{6,70},{7,71},{8,72},{9,... | collective-permute-start | bytes 1572872 | tf_op jit(solution)/shard_map/ppermute | solution.py:215
  17.2 4.7 %collective-permute-start.6 = (bf16[128,16,256]{2,1,0:T(8,128)(2,1)S(1)}, bf16[128,16,256]{2,1,0:T(8,128)(2,1)S(1)}, u32[]{:S(2)}, u32[]{:S(2)}) collective-permute-start(bf16[128,16,256]{2,1,0:T(8,128)(2,1)S(1)} %get-tuple-element.76), channel_id=1, source_target_pairs={{0,32},{1,33},{2,34},{3,35},{4,36},{5,37},{6,38},{7,39},{8,40},{9,... | collective-permute-start | bytes 3145736 | tf_op jit(solution)/shard_map/ppermute | solution.py:208
  17.9 5.1 %collective-permute-start.7 = (bf16[128,16,256]{2,1,0:T(8,128)(2,1)S(1)}, bf16[128,16,256]{2,1,0:T(8,128)(2,1)S(1)}, u32[]{:S(2)}, u32[]{:S(2)}) collective-permute-start(bf16[128,16,256]{2,1,0:T(8,128)(2,1)S(1)} %get-tuple-element.79), channel_id=1, source_target_pairs={{0,32},{1,33},{2,34},{3,35},{4,36},{5,37},{6,38},{7,39},{8,40},{9,... | collective-permute-start | bytes 3145736 | tf_op jit(solution)/shard_map/ppermute | solution.py:208
  18.2 9.3 %collective-permute-start.8 = (bf16[64,16,256]{2,1,0:T(8,128)(2,1)S(1)}, bf16[64,16,256]{2,1,0:T(8,128)(2,1)S(1)}, u32[]{:S(2)}, u32[]{:S(2)}) collective-permute-start(bf16[64,16,256]{2,1,0:T(8,128)(2,1)S(1)} %get-tuple-element.81), channel_id=1, source_target_pairs={{0,1},{1,0},{2,3},{3,2},{4,5},{5,4},{6,7},{7,6},{8,9},{9,8},{10,11... | collective-permute-start | bytes 1572872 | tf_op jit(solution)/shard_map/ppermute | solution.py:215
  20.3 10.3 %collective-permute-start.9 = (bf16[64,16,256]{2,1,0:T(8,128)(2,1)S(1)}, bf16[64,16,256]{2,1,0:T(8,128)(2,1)S(1)}, u32[]{:S(2)}, u32[]{:S(2)}) collective-permute-start(bf16[64,16,256]{2,1,0:T(8,128)(2,1)S(1)} %get-tuple-element.83), channel_id=1, source_target_pairs={{0,64},{1,65},{2,66},{3,67},{4,68},{5,69},{6,70},{7,71},{8,72},{9,... | collective-permute-start | bytes 1572872 | tf_op jit(solution)/shard_map/ppermute | solution.py:215
  22.0 13.2 %collective-permute-start.10 = (bf16[64,16,256]{2,1,0:T(8,128)(2,1)S(1)}, bf16[64,16,256]{2,1,0:T(8,128)(2,1)S(1)}, u32[]{:S(2)}, u32[]{:S(2)}) collective-permute-start(bf16[64,16,256]{2,1,0:T(8,128)(2,1)S(1)} %get-tuple-element.85), channel_id=1, source_target_pairs={{0,1},{1,0},{2,3},{3,2},{4,5},{5,4},{6,7},{7,6},{8,9},{9,8},{10,11... | collective-permute-start | bytes 1572872 | tf_op jit(solution)/shard_map/ppermute | solution.py:215
  23.2 15.0 %collective-permute-start.11 = (bf16[64,16,256]{2,1,0:T(8,128)(2,1)S(1)}, bf16[64,16,256]{2,1,0:T(8,128)(2,1)S(1)}, u32[]{:S(2)}, u32[]{:S(2)}) collective-permute-start(bf16[64,16,256]{2,1,0:T(8,128)(2,1)S(1)} %get-tuple-element.87), channel_id=1, source_target_pairs={{0,64},{1,65},{2,66},{3,67},{4,68},{5,69},{6,70},{7,71},{8,72},{9,... | collective-permute-start | bytes 1572872 | tf_op jit(solution)/shard_map/ppermute | solution.py:215
  27.7 12.9 %collective-permute-start.12 = (bf16[64,16,256]{2,1,0:T(8,128)(2,1)S(1)}, bf16[64,16,256]{2,1,0:T(8,128)(2,1)S(1)}, u32[]{:S(2)}, u32[]{:S(2)}) collective-permute-start(bf16[64,16,256]{2,1,0:T(8,128)(2,1)S(1)} %get-tuple-element.89), channel_id=1, source_target_pairs={{0,3},{1,2},{2,1},{3,0},{4,7},{5,6},{6,5},{7,4},{8,11},{9,10},{10,... | collective-permute-start | bytes 1572872 | tf_op jit(solution)/shard_map/ppermute | solution.py:215
  30.9 11.3 %collective-permute-start.13 = (bf16[64,16,256]{2,1,0:T(8,128)(2,1)S(1)}, bf16[64,16,256]{2,1,0:T(8,128)(2,1)S(1)}, u32[]{:S(2)}, u32[]{:S(2)}) collective-permute-start(bf16[64,16,256]{2,1,0:T(8,128)(2,1)S(1)} %get-tuple-element.91), channel_id=1, source_target_pairs={{0,192},{1,193},{2,194},{3,195},{4,196},{5,197},{6,198},{7,199},{8... | collective-permute-start | bytes 1572872 | tf_op jit(solution)/shard_map/ppermute | solution.py:215
  35.4 8.1 %collective-permute-start.14 = (bf16[32,16,256]{2,1,0:T(8,128)(2,1)S(1)}, bf16[32,16,256]{2,1,0:T(8,128)(2,1)S(1)}, u32[]{:S(2)}, u32[]{:S(2)}) collective-permute-start(bf16[32,16,256]{2,1,0:T(8,128)(2,1)S(1)} %get-tuple-element.93), channel_id=1, source_target_pairs={{0,3},{1,2},{2,1},{3,0},{4,7},{5,6},{6,5},{7,4},{8,11},{9,10},{10,... | collective-permute-start | bytes 786440 | tf_op jit(solution)/shard_map/ppermute | solution.py:215
  38.3 10.5 %collective-permute-start.15 = (bf16[32,16,256]{2,1,0:T(8,128)(2,1)S(1)}, bf16[32,16,256]{2,1,0:T(8,128)(2,1)S(1)}, u32[]{:S(2)}, u32[]{:S(2)}) collective-permute-start(bf16[32,16,256]{2,1,0:T(8,128)(2,1)S(1)} %get-tuple-element.95), channel_id=1, source_target_pairs={{0,192},{1,193},{2,194},{3,195},{4,196},{5,197},{6,198},{7,199},{8... | collective-permute-start | bytes 786440 | tf_op jit(solution)/shard_map/ppermute | solution.py:215
  40.9 8.9 %collective-permute-start.16 = (bf16[32,16,256]{2,1,0:T(8,128)(2,1)S(1)}, bf16[32,16,256]{2,1,0:T(8,128)(2,1)S(1)}, u32[]{:S(2)}, u32[]{:S(2)}) collective-permute-start(bf16[32,16,256]{2,1,0:T(8,128)(2,1)S(1)} %get-tuple-element.97), channel_id=1, source_target_pairs={{0,64},{1,65},{2,66},{3,67},{4,68},{5,69},{6,70},{7,71},{8,72},{9,... | collective-permute-start | bytes 786440 | tf_op jit(solution)/shard_map/ppermute | solution.py:215
  42.3 7.5 %collective-permute-start.17 = (bf16[32,16,256]{2,1,0:T(8,128)(2,1)S(1)}, bf16[32,16,256]{2,1,0:T(8,128)(2,1)S(1)}, u32[]{:S(2)}, u32[]{:S(2)}) collective-permute-start(bf16[32,16,256]{2,1,0:T(8,128)(2,1)S(1)} %get-tuple-element.98), channel_id=1, source_target_pairs={{0,1},{1,0},{2,3},{3,2},{4,5},{5,4},{6,7},{7,6},{8,9},{9,8},{10,11... | collective-permute-start | bytes 786440 | tf_op jit(solution)/shard_map/ppermute | solution.py:215
  43.5 6.3 %collective-permute-start.18 = (bf16[16,16,256]{2,1,0:T(8,128)(2,1)S(1)}, bf16[16,16,256]{2,1,0:T(8,128)(2,1)S(1)}, u32[]{:S(2)}, u32[]{:S(2)}) collective-permute-start(bf16[16,16,256]{2,1,0:T(8,128)(2,1)S(1)} %get-tuple-element.99), channel_id=1, source_target_pairs={{0,64},{1,65},{2,66},{3,67},{4,68},{5,69},{6,70},{7,71},{8,72},{9,... | collective-permute-start | bytes 393224 | tf_op jit(solution)/shard_map/ppermute | solution.py:215
  48.9 6.2 %collective-permute-start.19 = (bf16[16,16,256]{2,1,0:T(8,128)(2,1)S(1)}, bf16[16,16,256]{2,1,0:T(8,128)(2,1)S(1)}, u32[]{:S(2)}, u32[]{:S(2)}) collective-permute-start(bf16[16,16,256]{2,1,0:T(8,128)(2,1)S(1)} %get-tuple-element.101), channel_id=1, source_target_pairs={{0,1},{1,0},{2,3},{3,2},{4,5},{5,4},{6,7},{7,6},{8,9},{9,8},{10,11... | collective-permute-start | bytes 393224 | tf_op jit(solution)/shard_map/ppermute | solution.py:215
  49.9 7.0 %collective-permute-start.20 = (bf16[24,16,256]{2,1,0:T(8,128)(2,1)S(1)}, bf16[24,16,256]{2,1,0:T(8,128)(2,1)S(1)}, u32[]{:S(2)}, u32[]{:S(2)}) collective-permute-start(bf16[24,16,256]{2,1,0:T(8,128)(2,1)S(1)} %get-tuple-element.103), channel_id=1, source_target_pairs={{0,192},{1,193},{2,194},{3,195},{4,196},{5,197},{6,198},{7,199},{8... | collective-permute-start | bytes 589832 | tf_op jit(solution)/shard_map/ppermute | solution.py:215
  55.2 7.0 %collective-permute-start.21 = (bf16[24,16,256]{2,1,0:T(8,128)(2,1)S(1)}, bf16[24,16,256]{2,1,0:T(8,128)(2,1)S(1)}, u32[]{:S(2)}, u32[]{:S(2)}) collective-permute-start(bf16[24,16,256]{2,1,0:T(8,128)(2,1)S(1)} %get-tuple-element.104), channel_id=1, source_target_pairs={{0,3},{1,2},{2,1},{3,0},{4,7},{5,6},{6,5},{7,4},{8,11},{9,10},{10,... | collective-permute-start | bytes 589832 | tf_op jit(solution)/shard_map/ppermute | solution.py:215

commit v4 on v3

--- a/solution.py
+++ b/solution.py
@@ -13,7 +13,7 @@
 K = 256
 TERMS = 32
 ROWS = 32
-CHUNKS = (4, 4, 8, 16)
+CHUNKS = (4, 12, 8, 8)
 LATER_CHUNKS = (16, 16)
 
 VMEM = pl.BlockSpec(memory_space=pltpu.VMEM)

time: 83.5 us -> 83.7 us (level)
  no operation moved by 1% of the time
where the time goes in v4:
time: 83.7 us; the launch traced here: 83.5 us
  starting transfers between devices  27.7 us (33%)
  blocking collectives  20.2 us (24%)
  waiting for transfers between devices  18.8 us (22%)
  Pallas kernels  15.3 us (18%)
    ppermute x16, starting transfers between devices, swap(): return lax.ppermute(a, AXES, permutation(move))  25.7 us
    all_to_all x1, blocking collectives, body(): spread = lax.all_to_all(last_sends(token, parts), 'z', 0, 0, tiled=True)  20.2 us
    ppermute x16, waiting for transfers between devices, swap(): return lax.ppermute(a, AXES, permutation(move))  18.8 us
    pallas_call x2, Pallas kernels, later_products(): pl.pallas_call(functools.partial(later_kernel, vectors), in_specs=[ANY, S...  6.47 us
    pallas_call x1, Pallas kernels, first_products(): pl.pallas_call(first_kernel, in_specs=[SMEM, HBM, HBM, HBM], out_specs=[V...  5.8 us
    pallas_call x16, Pallas kernels, combine(): pl.pallas_call(functools.partial(combine_kernel, n, places), in_specs=[AN...  2.7 us
    ppermute x6, starting transfers between devices, core_swap(): lax.ppermute(a, AXES, permutation(lambda y, c, z, x: (y, 1 - c, z, x)))  2.01 us
  transfers between devices with their start and end apart: 22, of which 8 were waited for; matrix products, arithmetic and copies ran while one was open for 0% of the time, Pallas kernels for 11%

profile of v4, /device:TPU:6, one launch (start us, length us, event | category | flops | bytes accessed | tf_op | source)
XLA Modules:
  0.0 83.5 jit_solution(8591235005351778718)
XLA Ops:
  0.0 0.7 copy-done
  0.7 5.8 %first_products.1 = (bf16[128,16,256]{2,1,0:T(8,128)(2,1)S(1)}, bf16[128,16,256]{2,1,0:T(8,128)(2,1)S(1)}, bf16[128,16,256]{2,1,0:T(8,128)(2,1)S(1)}, bf16[128,1...) custom-call(s32[32]{0:T(128)S(1)} %bitcast.2, ...), custom_call_target="tpu_custom_call" | custom-call | flops 1 | bytes 1 | tf_op jit(solution)/shard_map/first_products/pallas_call | solution.py:121
  6.5 0.1 collective-permute-start
  6.6 0.5 collective-permute-start.1
  7.1 3.2 %later_products.2 = (bf16[128,16,256]{2,1,0:T(8,128)(2,1)S(1)}, bf16[128,16,256]{2,1,0:T(8,128)(2,1)S(1)}, bf16[128,16,256]{2,1,0:T(8,128)(2,1)S(1)}, bf16[128,16,256]{2,1,0:T(8,128)(2,1)S(1)}, f32[8,128]{1,0:T(8,128)S(1)}) custom-call(f32[8,128]{1,0:T(8,128)S(1)} %get-tuple-element.55.after_ref, s32[32]{0:T(128)S(1)} %bitcast.3, ...), custom_call_target="tpu_custom_call" | custom-call | flops 1 | bytes 1 | tf_op jit(solution)/shard_map/later_products/pallas_call | solution.py:134
  10.3 0.2 collective-permute-start.2
  10.5 0.4 collective-permute-start.3
  10.9 0.0 collective-permute-done.refs_2_
  10.9 0.2 combine.16
  11.1 0.9 %collective-permute-start.4 = (bf16[64,16,256]{2,1,0:T(8,128)(2,1)S(1)}, bf16[64,16,256]{2,1,0:T(8,128)(2,1)S(1)}, u32[]{:S(2)}, u32[]{:S(2)}) collective-permute-start(bf16[64,16,256]{2,1,0:T(8,128)(2,1)S(1)} %get-tuple-element.73), channel_id=1, source_target_pairs={{0,1},{1,0},{2,3},{3,2},{4,5},{5,4},{6,7},{7,6},{8,9},{9,8},{10,11... | collective-permute-start | bytes 1572872 | tf_op jit(solution)/shard_map/ppermute | solution.py:215
  12.0 0.0 collective-permute-done.1.refs_2_.refs_8_
  12.0 0.2 combine.17
  12.2 1.8 %collective-permute-start.5 = (bf16[64,16,256]{2,1,0:T(8,128)(2,1)S(1)}, bf16[64,16,256]{2,1,0:T(8,128)(2,1)S(1)}, u32[]{:S(2)}, u32[]{:S(2)}) collective-permute-start(bf16[64,16,256]{2,1,0:T(8,128)(2,1)S(1)} %get-tuple-element.74), channel_id=1, source_target_pairs={{0,64},{1,65},{2,66},{3,67},{4,68},{5,69},{6,70},{7,71},{8,72},{9,... | collective-permute-start | bytes 1572872 | tf_op jit(solution)/shard_map/ppermute | solution.py:215
  14.0 3.2 %later_products.3 = (bf16[128,16,256]{2,1,0:T(8,128)(2,1)S(1)}, bf16[128,16,256]{2,1,0:T(8,128)(2,1)S(1)}, bf16[128,16,256]{2,1,0:T(8,128)(2,1)S(1)}, bf16[128,16,256]{2,1,0:T(8,128)(2,1)S(1)}, f32[8,128]{1,0:T(8,128)S(1)}) custom-call(f32[8,128]{1,0:T(8,128)S(1)} %get-tuple-element.65.after_ref, s32[32]{0:T(128)S(1)} %bitcast.4, ...), custom_call_target="tpu_custom_call" | custom-call | flops 1 | bytes 1 | tf_op jit(solution)/shard_map/later_products/pallas_call | solution.py:134
  17.3 0.7 collective-permute-start.6
  18.0 0.0 collective-permute-done.2.refs_2_.refs_5_.refs_6_.refs_7_.refs_14_
  18.0 0.1 collective-permute-start.7
  18.1 0.2 combine.18
  18.3 0.0 collective-permute-done.3.refs_2_.refs_5_.refs_6_.refs_7_.refs_17_
  18.3 1.0 %collective-permute-start.8 = (bf16[64,16,256]{2,1,0:T(8,128)(2,1)S(1)}, bf16[64,16,256]{2,1,0:T(8,128)(2,1)S(1)}, u32[]{:S(2)}, u32[]{:S(2)}) collective-permute-start(bf16[64,16,256]{2,1,0:T(8,128)(2,1)S(1)} %get-tuple-element.81), channel_id=1, source_target_pairs={{0,1},{1,0},{2,3},{3,2},{4,5},{5,4},{6,7},{7,6},{8,9},{9,8},{10,11... | collective-permute-start | bytes 1572872 | tf_op jit(solution)/shard_map/ppermute | solution.py:215
  19.4 0.2 combine.19
  19.5 0.8 collective-permute-done.4.got_ref.refs_3_
  20.4 1.6 %collective-permute-start.9 = (bf16[64,16,256]{2,1,0:T(8,128)(2,1)S(1)}, bf16[64,16,256]{2,1,0:T(8,128)(2,1)S(1)}, u32[]{:S(2)}, u32[]{:S(2)}) collective-permute-start(bf16[64,16,256]{2,1,0:T(8,128)(2,1)S(1)} %get-tuple-element.83), channel_id=1, source_target_pairs={{0,64},{1,65},{2,66},{3,67},{4,68},{5,69},{6,70},{7,71},{8,72},{9,... | collective-permute-start | bytes 1572872 | tf_op jit(solution)/shard_map/ppermute | solution.py:215
  21.9 0.0 collective-permute-done.5.got_ref.refs_3_.refs_9_
  21.9 0.0 collective-permute-done.6.refs_2_.refs_10_.refs_20_
  21.9 0.2 combine.20
  22.1 1.0 %collective-permute-start.10 = (bf16[64,16,256]{2,1,0:T(8,128)(2,1)S(1)}, bf16[64,16,256]{2,1,0:T(8,128)(2,1)S(1)}, u32[]{:S(2)}, u32[]{:S(2)}) collective-permute-start(bf16[64,16,256]{2,1,0:T(8,128)(2,1)S(1)} %get-tuple-element.85), channel_id=1, source_target_pairs={{0,1},{1,0},{2,3},{3,2},{4,5},{5,4},{6,7},{7,6},{8,9},{9,8},{10,11... | collective-permute-start | bytes 1572872 | tf_op jit(solution)/shard_map/ppermute | solution.py:215
  23.1 0.2 combine.21
  23.3 1.7 %collective-permute-start.11 = (bf16[64,16,256]{2,1,0:T(8,128)(2,1)S(1)}, bf16[64,16,256]{2,1,0:T(8,128)(2,1)S(1)}, u32[]{:S(2)}, u32[]{:S(2)}) collective-permute-start(bf16[64,16,256]{2,1,0:T(8,128)(2,1)S(1)} %get-tuple-element.87), channel_id=1, source_target_pairs={{0,64},{1,65},{2,66},{3,67},{4,68},{5,69},{6,70},{7,71},{8,72},{9,... | collective-permute-start | bytes 1572872 | tf_op jit(solution)/shard_map/ppermute | solution.py:215
  25.0 2.6 %collective-permute-done.8.refs_6_.refs_7_.refs_8_.refs_15_ = bf16[64,16,256]{2,1,0:T(8,128)(2,1)S(1)} collective-permute-done((bf16[64,16,256]{2,1,0:T(8,128)(2,1)S(1)}, bf16[64,16,256]{2,1,0:T(8,128)(2,1)S(1)}, u32[]{:S(2)}, u32[]{:S(2)}) %collective-permute-start.8) | collective-permute-done | bytes 524320 | tf_op jit(solution)/shard_map/ppermute | solution.py:215
  27.6 0.3 combine.22
  27.9 2.8 %collective-permute-start.12 = (bf16[64,16,256]{2,1,0:T(8,128)(2,1)S(1)}, bf16[64,16,256]{2,1,0:T(8,128)(2,1)S(1)}, u32[]{:S(2)}, u32[]{:S(2)}) collective-permute-start(bf16[64,16,256]{2,1,0:T(8,128)(2,1)S(1)} %get-tuple-element.89), channel_id=1, source_target_pairs={{0,3},{1,2},{2,1},{3,0},{4,7},{5,6},{6,5},{7,4},{8,11},{9,10},{10,... | collective-permute-start | bytes 1572872 | tf_op jit(solution)/shard_map/ppermute | solution.py:215
  30.7 0.3 combine.23
  31.0 1.9 %collective-permute-start.13 = (bf16[64,16,256]{2,1,0:T(8,128)(2,1)S(1)}, bf16[64,16,256]{2,1,0:T(8,128)(2,1)S(1)}, u32[]{:S(2)}, u32[]{:S(2)}) collective-permute-start(bf16[64,16,256]{2,1,0:T(8,128)(2,1)S(1)} %get-tuple-element.91), channel_id=1, source_target_pairs={{0,192},{1,193},{2,194},{3,195},{4,196},{5,197},{6,198},{7,199},{8... | collective-permute-start | bytes 1572872 | tf_op jit(solution)/shard_map/ppermute | solution.py:215
  32.9 2.4 %collective-permute-done.10.refs_3_.refs_11_.refs_21_ = bf16[64,16,256]{2,1,0:T(8,128)(2,1)S(1)} collective-permute-done((bf16[64,16,256]{2,1,0:T(8,128)(2,1)S(1)}, bf16[64,16,256]{2,1,0:T(8,128)(2,1)S(1)}, u32[]{:S(2)}, u32[]{:S(2)}) %collective-permute-start.10) | collective-permute-done | bytes 524320 | tf_op jit(solution)/shard_map/ppermute | solution.py:215
  35.3 0.1 combine.24
  35.5 2.8 %collective-permute-start.14 = (bf16[32,16,256]{2,1,0:T(8,128)(2,1)S(1)}, bf16[32,16,256]{2,1,0:T(8,128)(2,1)S(1)}, u32[]{:S(2)}, u32[]{:S(2)}) collective-permute-start(bf16[32,16,256]{2,1,0:T(8,128)(2,1)S(1)} %get-tuple-element.93), channel_id=1, source_target_pairs={{0,3},{1,2},{2,1},{3,0},{4,7},{5,6},{6,5},{7,4},{8,11},{9,10},{10,... | collective-permute-start | bytes 786440 | tf_op jit(solution)/shard_map/ppermute | solution.py:215
  38.3 0.0 collective-permute-done.11.refs_3_.refs_11_.refs_26_
  38.3 0.1 combine.25
  38.5 2.3 %collective-permute-start.15 = (bf16[32,16,256]{2,1,0:T(8,128)(2,1)S(1)}, bf16[32,16,256]{2,1,0:T(8,128)(2,1)S(1)}, u32[]{:S(2)}, u32[]{:S(2)}) collective-permute-start(bf16[32,16,256]{2,1,0:T(8,128)(2,1)S(1)} %get-tuple-element.95), channel_id=1, source_target_pairs={{0,192},{1,193},{2,194},{3,195},{4,196},{5,197},{6,198},{7,199},{8... | collective-permute-start | bytes 786440 | tf_op jit(solution)/shard_map/ppermute | solution.py:215
  40.8 0.0 collective-permute-done.12.refs_4_
  40.8 0.2 combine.26
  41.0 0.7 collective-permute-start.16
  41.6 0.6 collective-permute-done.13.refs_4_.refs_10_
  42.2 0.2 combine.27
  42.4 1.1 %collective-permute-start.17 = (bf16[32,16,256]{2,1,0:T(8,128)(2,1)S(1)}, bf16[32,16,256]{2,1,0:T(8,128)(2,1)S(1)}, u32[]{:S(2)}, u32[]{:S(2)}) collective-permute-start(bf16[32,16,256]{2,1,0:T(8,128)(2,1)S(1)} %get-tuple-element.98), channel_id=1, source_target_pairs={{0,1},{1,0},{2,3},{3,2},{4,5},{5,4},{6,7},{7,6},{8,9},{9,8},{10,11... | collective-permute-start | bytes 786440 | tf_op jit(solution)/shard_map/ppermute | solution.py:215
  43.5 0.1 combine.28
  43.6 1.6 %collective-permute-start.18 = (bf16[16,16,256]{2,1,0:T(8,128)(2,1)S(1)}, bf16[16,16,256]{2,1,0:T(8,128)(2,1)S(1)}, u32[]{:S(2)}, u32[]{:S(2)}) collective-permute-start(bf16[16,16,256]{2,1,0:T(8,128)(2,1)S(1)} %get-tuple-element.99), channel_id=1, source_target_pairs={{0,64},{1,65},{2,66},{3,67},{4,68},{5,69},{6,70},{7,71},{8,72},{9,... | collective-permute-start | bytes 393224 | tf_op jit(solution)/shard_map/ppermute | solution.py:215
  45.3 3.7 %collective-permute-done.15.refs_4_.refs_12_.refs_27_ = bf16[32,16,256]{2,1,0:T(8,128)(2,1)S(1)} collective-permute-done((bf16[32,16,256]{2,1,0:T(8,128)(2,1)S(1)}, bf16[32,16,256]{2,1,0:T(8,128)(2,1)S(1)}, u32[]{:S(2)}, u32[]{:S(2)}) %collective-permute-start.15) | collective-permute-done | bytes 262176 | tf_op jit(solution)/shard_map/ppermute | solution.py:215
  48.9 0.1 combine.29
  49.0 0.8 %collective-permute-start.19 = (bf16[16,16,256]{2,1,0:T(8,128)(2,1)S(1)}, bf16[16,16,256]{2,1,0:T(8,128)(2,1)S(1)}, u32[]{:S(2)}, u32[]{:S(2)}) collective-permute-start(bf16[16,16,256]{2,1,0:T(8,128)(2,1)S(1)} %get-tuple-element.101), channel_id=1, source_target_pairs={{0,1},{1,0},{2,3},{3,2},{4,5},{5,4},{6,7},{7,6},{8,9},{9,8},{10,11... | collective-permute-start | bytes 393224 | tf_op jit(solution)/shard_map/ppermute | solution.py:215
  49.9 0.0 collective-permute-done.16.got_ref.refs_5_
  49.9 0.0 collective-permute-done.17.got_ref.refs_5_.refs_11_
  49.9 0.0 collective-permute-done.18.refs_13_.refs_23_
  49.9 0.2 combine.30
  50.1 3.3 %collective-permute-start.20 = (bf16[24,16,256]{2,1,0:T(8,128)(2,1)S(1)}, bf16[24,16,256]{2,1,0:T(8,128)(2,1)S(1)}, u32[]{:S(2)}, u32[]{:S(2)}) collective-permute-start(bf16[24,16,256]{2,1,0:T(8,128)(2,1)S(1)} %get-tuple-element.103), channel_id=1, source_target_pairs={{0,192},{1,193},{2,194},{3,195},{4,196},{5,197},{6,198},{7,199},{8... | collective-permute-start | bytes 589832 | tf_op jit(solution)/shard_map/ppermute | solution.py:215
  53.4 1.8 %collective-permute-done.19.refs_13_.refs_28_ = bf16[16,16,256]{2,1,0:T(8,128)(2,1)S(1)} collective-permute-done((bf16[16,16,256]{2,1,0:T(8,128)(2,1)S(1)}, bf16[16,16,256]{2,1,0:T(8,128)(2,1)S(1)}, u32[]{:S(2)}, u32[]{:S(2)}) %collective-permute-start.19) | collective-permute-done | bytes 131104 | tf_op jit(solution)/shard_map/ppermute | solution.py:215
  55.2 0.1 combine.31
  55.3 0.1 collective-permute-start.21
  55.4 1.6 %collective-permute-done.20.got_ref.refs_6_ = bf16[24,16,256]{2,1,0:T(8,128)(2,1)S(1)} collective-permute-done((bf16[24,16,256]{2,1,0:T(8,128)(2,1)S(1)}, bf16[24,16,256]{2,1,0:T(8,128)(2,1)S(1)}, u32[]{:S(2)}, u32[]{:S(2)}) %collective-permute-start.20) | collective-permute-done | bytes 196640 | tf_op jit(solution)/shard_map/ppermute | solution.py:215
  57.0 5.3 %collective-permute-done.21.refs_12_ = bf16[24,16,256]{2,1,0:T(8,128)(2,1)S(1)} collective-permute-done((bf16[24,16,256]{2,1,0:T(8,128)(2,1)S(1)}, bf16[24,16,256]{2,1,0:T(8,128)(2,1)S(1)}, u32[]{:S(2)}, u32[]{:S(2)}) %collective-permute-start.21) | collective-permute-done | bytes 196640 | tf_op jit(solution)/shard_map/ppermute | solution.py:215
  62.3 0.3 last_sends.1
  62.7 20.2 %all_to_all.5 = bf16[8,3,32,256]{3,2,1,0:T(8,128)(2,1)S(1)} all-to-all(bf16[8,3,32,256]{3,2,1,0:T(8,128)(2,1)S(1)} %last_sends.1), channel_id=1, replica_groups=mesh['y'=4,'c'=2,'z'=8,'x'=4] {'z'}, dimensions={0} | all-to-all | bytes 786432 | tf_op jit(solution)/shard_map/all_to_all | solution.py:280
  82.8 0.7 convert_reduce_fusion
  (9 shorter events, 0.0 us)
Async XLA Ops:
  0.0 0.7 copy-start
  6.5 4.4 %collective-permute-start = (bf16[128,16,256]{2,1,0:T(8,128)(2,1)S(1)}, bf16[128,16,256]{2,1,0:T(8,128)(2,1)S(1)}, u32[]{:S(2)}, u32[]{:S(2)}) collective-permute-start(bf16[128,16,256]{2,1,0:T(8,128)(2,1)S(1)} %get-tuple-element.61), channel_id=1, source_target_pairs={{0,32},{1,33},{2,34},{3,35},{4,36},{5,37},{6,38},{7,39},{8,40},{9,... | collective-permute-start | bytes 3145736 | tf_op jit(solution)/shard_map/ppermute | solution.py:208
  6.6 5.4 %collective-permute-start.1 = (bf16[128,16,256]{2,1,0:T(8,128)(2,1)S(1)}, bf16[128,16,256]{2,1,0:T(8,128)(2,1)S(1)}, u32[]{:S(2)}, u32[]{:S(2)}) collective-permute-start(bf16[128,16,256]{2,1,0:T(8,128)(2,1)S(1)} %get-tuple-element.64), channel_id=1, source_target_pairs={{0,32},{1,33},{2,34},{3,35},{4,36},{5,37},{6,38},{7,39},{8,40},{9,... | collective-permute-start | bytes 3145736 | tf_op jit(solution)/shard_map/ppermute | solution.py:208
  10.3 7.7 %collective-permute-start.2 = (bf16[128,16,256]{2,1,0:T(8,128)(2,1)S(1)}, bf16[128,16,256]{2,1,0:T(8,128)(2,1)S(1)}, u32[]{:S(2)}, u32[]{:S(2)}) collective-permute-start(bf16[128,16,256]{2,1,0:T(8,128)(2,1)S(1)} %get-tuple-element.68), channel_id=1, source_target_pairs={{0,32},{1,33},{2,34},{3,35},{4,36},{5,37},{6,38},{7,39},{8,40},{9,... | collective-permute-start | bytes 3145736 | tf_op jit(solution)/shard_map/ppermute | solution.py:208
  10.5 7.8 %collective-permute-start.3 = (bf16[128,16,256]{2,1,0:T(8,128)(2,1)S(1)}, bf16[128,16,256]{2,1,0:T(8,128)(2,1)S(1)}, u32[]{:S(2)}, u32[]{:S(2)}) collective-permute-start(bf16[128,16,256]{2,1,0:T(8,128)(2,1)S(1)} %get-tuple-element.71), channel_id=1, source_target_pairs={{0,32},{1,33},{2,34},{3,35},{4,36},{5,37},{6,38},{7,39},{8,40},{9,... | collective-permute-start | bytes 3145736 | tf_op jit(solution)/shard_map/ppermute | solution.py:208
  11.1 9.3 %collective-permute-start.4 = (bf16[64,16,256]{2,1,0:T(8,128)(2,1)S(1)}, bf16[64,16,256]{2,1,0:T(8,128)(2,1)S(1)}, u32[]{:S(2)}, u32[]{:S(2)}) collective-permute-start(bf16[64,16,256]{2,1,0:T(8,128)(2,1)S(1)} %get-tuple-element.73), channel_id=1, source_target_pairs={{0,1},{1,0},{2,3},{3,2},{4,5},{5,4},{6,7},{7,6},{8,9},{9,8},{10,11... | collective-permute-start | bytes 1572872 | tf_op jit(solution)/shard_map/ppermute | solution.py:215
  12.2 9.7 %collective-permute-start.5 = (bf16[64,16,256]{2,1,0:T(8,128)(2,1)S(1)}, bf16[64,16,256]{2,1,0:T(8,128)(2,1)S(1)}, u32[]{:S(2)}, u32[]{:S(2)}) collective-permute-start(bf16[64,16,256]{2,1,0:T(8,128)(2,1)S(1)} %get-tuple-element.74), channel_id=1, source_target_pairs={{0,64},{1,65},{2,66},{3,67},{4,68},{5,69},{6,70},{7,71},{8,72},{9,... | collective-permute-start | bytes 1572872 | tf_op jit(solution)/shard_map/ppermute | solution.py:215
  17.3 4.7 %collective-permute-start.6 = (bf16[128,16,256]{2,1,0:T(8,128)(2,1)S(1)}, bf16[128,16,256]{2,1,0:T(8,128)(2,1)S(1)}, u32[]{:S(2)}, u32[]{:S(2)}) collective-permute-start(bf16[128,16,256]{2,1,0:T(8,128)(2,1)S(1)} %get-tuple-element.76), channel_id=1, source_target_pairs={{0,32},{1,33},{2,34},{3,35},{4,36},{5,37},{6,38},{7,39},{8,40},{9,... | collective-permute-start | bytes 3145736 | tf_op jit(solution)/shard_map/ppermute | solution.py:208
  18.0 5.1 %collective-permute-start.7 = (bf16[128,16,256]{2,1,0:T(8,128)(2,1)S(1)}, bf16[128,16,256]{2,1,0:T(8,128)(2,1)S(1)}, u32[]{:S(2)}, u32[]{:S(2)}) collective-permute-start(bf16[128,16,256]{2,1,0:T(8,128)(2,1)S(1)} %get-tuple-element.79), channel_id=1, source_target_pairs={{0,32},{1,33},{2,34},{3,35},{4,36},{5,37},{6,38},{7,39},{8,40},{9,... | collective-permute-start | bytes 3145736 | tf_op jit(solution)/shard_map/ppermute | solution.py:208
  18.3 9.3 %collective-permute-start.8 = (bf16[64,16,256]{2,1,0:T(8,128)(2,1)S(1)}, bf16[64,16,256]{2,1,0:T(8,128)(2,1)S(1)}, u32[]{:S(2)}, u32[]{:S(2)}) collective-permute-start(bf16[64,16,256]{2,1,0:T(8,128)(2,1)S(1)} %get-tuple-element.81), channel_id=1, source_target_pairs={{0,1},{1,0},{2,3},{3,2},{4,5},{5,4},{6,7},{7,6},{8,9},{9,8},{10,11... | collective-permute-start | bytes 1572872 | tf_op jit(solution)/shard_map/ppermute | solution.py:215
  20.4 10.3 %collective-permute-start.9 = (bf16[64,16,256]{2,1,0:T(8,128)(2,1)S(1)}, bf16[64,16,256]{2,1,0:T(8,128)(2,1)S(1)}, u32[]{:S(2)}, u32[]{:S(2)}) collective-permute-start(bf16[64,16,256]{2,1,0:T(8,128)(2,1)S(1)} %get-tuple-element.83), channel_id=1, source_target_pairs={{0,64},{1,65},{2,66},{3,67},{4,68},{5,69},{6,70},{7,71},{8,72},{9,... | collective-permute-start | bytes 1572872 | tf_op jit(solution)/shard_map/ppermute | solution.py:215
  22.1 13.2 %collective-permute-start.10 = (bf16[64,16,256]{2,1,0:T(8,128)(2,1)S(1)}, bf16[64,16,256]{2,1,0:T(8,128)(2,1)S(1)}, u32[]{:S(2)}, u32[]{:S(2)}) collective-permute-start(bf16[64,16,256]{2,1,0:T(8,128)(2,1)S(1)} %get-tuple-element.85), channel_id=1, source_target_pairs={{0,1},{1,0},{2,3},{3,2},{4,5},{5,4},{6,7},{7,6},{8,9},{9,8},{10,11... | collective-permute-start | bytes 1572872 | tf_op jit(solution)/shard_map/ppermute | solution.py:215
  23.3 15.0 %collective-permute-start.11 = (bf16[64,16,256]{2,1,0:T(8,128)(2,1)S(1)}, bf16[64,16,256]{2,1,0:T(8,128)(2,1)S(1)}, u32[]{:S(2)}, u32[]{:S(2)}) collective-permute-start(bf16[64,16,256]{2,1,0:T(8,128)(2,1)S(1)} %get-tuple-element.87), channel_id=1, source_target_pairs={{0,64},{1,65},{2,66},{3,67},{4,68},{5,69},{6,70},{7,71},{8,72},{9,... | collective-permute-start | bytes 1572872 | tf_op jit(solution)/shard_map/ppermute | solution.py:215
  27.9 12.9 %collective-permute-start.12 = (bf16[64,16,256]{2,1,0:T(8,128)(2,1)S(1)}, bf16[64,16,256]{2,1,0:T(8,128)(2,1)S(1)}, u32[]{:S(2)}, u32[]{:S(2)}) collective-permute-start(bf16[64,16,256]{2,1,0:T(8,128)(2,1)S(1)} %get-tuple-element.89), channel_id=1, source_target_pairs={{0,3},{1,2},{2,1},{3,0},{4,7},{5,6},{6,5},{7,4},{8,11},{9,10},{10,... | collective-permute-start | bytes 1572872 | tf_op jit(solution)/shard_map/ppermute | solution.py:215
  31.0 11.3 %collective-permute-start.13 = (bf16[64,16,256]{2,1,0:T(8,128)(2,1)S(1)}, bf16[64,16,256]{2,1,0:T(8,128)(2,1)S(1)}, u32[]{:S(2)}, u32[]{:S(2)}) collective-permute-start(bf16[64,16,256]{2,1,0:T(8,128)(2,1)S(1)} %get-tuple-element.91), channel_id=1, source_target_pairs={{0,192},{1,193},{2,194},{3,195},{4,196},{5,197},{6,198},{7,199},{8... | collective-permute-start | bytes 1572872 | tf_op jit(solution)/shard_map/ppermute | solution.py:215
  35.5 8.1 %collective-permute-start.14 = (bf16[32,16,256]{2,1,0:T(8,128)(2,1)S(1)}, bf16[32,16,256]{2,1,0:T(8,128)(2,1)S(1)}, u32[]{:S(2)}, u32[]{:S(2)}) collective-permute-start(bf16[32,16,256]{2,1,0:T(8,128)(2,1)S(1)} %get-tuple-element.93), channel_id=1, source_target_pairs={{0,3},{1,2},{2,1},{3,0},{4,7},{5,6},{6,5},{7,4},{8,11},{9,10},{10,... | collective-permute-start | bytes 786440 | tf_op jit(solution)/shard_map/ppermute | solution.py:215
  38.5 10.5 %collective-permute-start.15 = (bf16[32,16,256]{2,1,0:T(8,128)(2,1)S(1)}, bf16[32,16,256]{2,1,0:T(8,128)(2,1)S(1)}, u32[]{:S(2)}, u32[]{:S(2)}) collective-permute-start(bf16[32,16,256]{2,1,0:T(8,128)(2,1)S(1)} %get-tuple-element.95), channel_id=1, source_target_pairs={{0,192},{1,193},{2,194},{3,195},{4,196},{5,197},{6,198},{7,199},{8... | collective-permute-start | bytes 786440 | tf_op jit(solution)/shard_map/ppermute | solution.py:215
  41.0 8.9 %collective-permute-start.16 = (bf16[32,16,256]{2,1,0:T(8,128)(2,1)S(1)}, bf16[32,16,256]{2,1,0:T(8,128)(2,1)S(1)}, u32[]{:S(2)}, u32[]{:S(2)}) collective-permute-start(bf16[32,16,256]{2,1,0:T(8,128)(2,1)S(1)} %get-tuple-element.97), channel_id=1, source_target_pairs={{0,64},{1,65},{2,66},{3,67},{4,68},{5,69},{6,70},{7,71},{8,72},{9,... | collective-permute-start | bytes 786440 | tf_op jit(solution)/shard_map/ppermute | solution.py:215
  42.4 7.5 %collective-permute-start.17 = (bf16[32,16,256]{2,1,0:T(8,128)(2,1)S(1)}, bf16[32,16,256]{2,1,0:T(8,128)(2,1)S(1)}, u32[]{:S(2)}, u32[]{:S(2)}) collective-permute-start(bf16[32,16,256]{2,1,0:T(8,128)(2,1)S(1)} %get-tuple-element.98), channel_id=1, source_target_pairs={{0,1},{1,0},{2,3},{3,2},{4,5},{5,4},{6,7},{7,6},{8,9},{9,8},{10,11... | collective-permute-start | bytes 786440 | tf_op jit(solution)/shard_map/ppermute | solution.py:215
  43.6 6.3 %collective-permute-start.18 = (bf16[16,16,256]{2,1,0:T(8,128)(2,1)S(1)}, bf16[16,16,256]{2,1,0:T(8,128)(2,1)S(1)}, u32[]{:S(2)}, u32[]{:S(2)}) collective-permute-start(bf16[16,16,256]{2,1,0:T(8,128)(2,1)S(1)} %get-tuple-element.99), channel_id=1, source_target_pairs={{0,64},{1,65},{2,66},{3,67},{4,68},{5,69},{6,70},{7,71},{8,72},{9,... | collective-permute-start | bytes 393224 | tf_op jit(solution)/shard_map/ppermute | solution.py:215
  49.0 6.2 %collective-permute-start.19 = (bf16[16,16,256]{2,1,0:T(8,128)(2,1)S(1)}, bf16[16,16,256]{2,1,0:T(8,128)(2,1)S(1)}, u32[]{:S(2)}, u32[]{:S(2)}) collective-permute-start(bf16[16,16,256]{2,1,0:T(8,128)(2,1)S(1)} %get-tuple-element.101), channel_id=1, source_target_pairs={{0,1},{1,0},{2,3},{3,2},{4,5},{5,4},{6,7},{7,6},{8,9},{9,8},{10,11... | collective-permute-start | bytes 393224 | tf_op jit(solution)/shard_map/ppermute | solution.py:215
  50.1 7.0 %collective-permute-start.20 = (bf16[24,16,256]{2,1,0:T(8,128)(2,1)S(1)}, bf16[24,16,256]{2,1,0:T(8,128)(2,1)S(1)}, u32[]{:S(2)}, u32[]{:S(2)}) collective-permute-start(bf16[24,16,256]{2,1,0:T(8,128)(2,1)S(1)} %get-tuple-element.103), channel_id=1, source_target_pairs={{0,192},{1,193},{2,194},{3,195},{4,196},{5,197},{6,198},{7,199},{8... | collective-permute-start | bytes 589832 | tf_op jit(solution)/shard_map/ppermute | solution.py:215
  55.3 7.0 %collective-permute-start.21 = (bf16[24,16,256]{2,1,0:T(8,128)(2,1)S(1)}, bf16[24,16,256]{2,1,0:T(8,128)(2,1)S(1)}, u32[]{:S(2)}, u32[]{:S(2)}) collective-permute-start(bf16[24,16,256]{2,1,0:T(8,128)(2,1)S(1)} %get-tuple-element.104), channel_id=1, source_target_pairs={{0,3},{1,2},{2,1},{3,0},{4,7},{5,6},{6,5},{7,4},{8,11},{9,10},{10,... | collective-permute-start | bytes 589832 | tf_op jit(solution)/shard_map/ppermute | solution.py:215
